TPU v7x, 128 devices: a whole 4x4x4 slice. The times are simulated.
128 devices in a mesh: blk: 64 (over y, z, x_lo, core), rep: 2 (over x_hi).
Axes of the slice: x: 4 (x_hi: 2, x_lo: 2; x = x_hi * 2 + x_lo), y: 4, z: 4, core: 2. Of those that a mesh axis runs over, the one named last changes fastest.
Arguments:
- features: float32 [16384, 128], P('blk'), may hold values from -6 to 6
- weight: float32 [128, 256], replicated, may hold values from -0.5 to 0.5
- tile_values: float32 [64, 64, 3, 128, 128], P('blk'), may hold values from -0.0625 to 0.0625
- tile_pos: int32 [64, 64, 3], P('blk'), may hold values from 0 to 3, as said below
- tile_counts: int32 [64, 64], P('blk'), may hold values from 0 to 3, as said below
- out_grad: float32 [16384, 256], P('blk'), may hold values from -6 to 6
Outputs:
- output: float32 [16384, 256], P('blk')
- feature_grad: float32 [16384, 128], P('blk')
- weight_grad: float32 [128, 256], replicated
Inputs may be any that keep to these rules, and one draw needn't show every extreme that they name: `tile_pos`: the 3 positions of one pair of blocks are different. `tile_counts`: every diagonal pair (b, b) holds 3 live tiles.
All inputs are finite; a program needn't handle non-finite values.
Results may differ from a plain program's by a relative error of at most 0.0003.
Values sent between devices are 32-bit elements; how exact they have to be, the bound alone decides.
A program may use at most 64 MiB of HBM per device.

v0:
```python
import math

import jax
import jax.numpy as jnp
from jax import lax
from jax.sharding import PartitionSpec as P

HIGHEST = lax.Precision.HIGHEST


def passed_along(x, axis, by):
    count = lax.axis_size(axis)
    return lax.ppermute(x, axis, [(i, (i + by) % count) for i in range(count)])


def shift_one(block_data):
    return passed_along(block_data, "blk", 1)


def half_turn(block_data):
    return passed_along(block_data, "blk", lax.axis_size("blk") // 2)


def replica_total(partial_value):
    return lax.psum(partial_value, "rep")


def weight_total(left_side, right_side, node_count):
    partial_value = jnp.einsum("nf,nd->fd", left_side, right_side, precision=HIGHEST)
    return lax.psum(partial_value, "blk") / math.sqrt(node_count)


def pick_pair(tile_values, tile_pos, tile_counts, column):
    values = lax.dynamic_index_in_dim(tile_values[0], column, 0, keepdims=False)
    positions = lax.dynamic_index_in_dim(tile_pos[0], column, 0, keepdims=False)
    live_count = lax.dynamic_index_in_dim(tile_counts[0], column, 0, keepdims=False)
    return (values, positions, live_count)


def pair_rows(values, positions, live_count, held_block):
    tile_size = values.shape[-1]
    slot_count = values.shape[0]
    feature_width = held_block.shape[1]
    tile_rows = held_block.shape[0] // tile_size
    tile_grid = held_block.reshape(tile_rows, tile_size, feature_width)
    picked = jnp.take(tile_grid, positions % tile_rows, axis=0)
    active = (jnp.arange(slot_count) < live_count).astype(jnp.float32)
    product = jnp.einsum("sij,sjf->sif", values, picked, precision=HIGHEST)
    placing = (positions[:, None] // tile_rows == jnp.arange(tile_rows)[None, :]).astype(
        jnp.float32
    ) * active[:, None]
    placed = jnp.einsum("st,sif->tif", placing, product, precision=HIGHEST)
    return placed.reshape(tile_rows * tile_size, feature_width)


def pair_columns(values, positions, live_count, gradients):
    tile_size = values.shape[-1]
    slot_count = values.shape[0]
    feature_width = gradients.shape[1]
    tile_rows = gradients.shape[0] // tile_size
    tile_grid = gradients.reshape(tile_rows, tile_size, feature_width)
    picked = jnp.take(tile_grid, positions // tile_rows, axis=0)
    active = (jnp.arange(slot_count) < live_count).astype(jnp.float32)
    product = jnp.einsum("sij,sif->sjf", values, picked, precision=HIGHEST)
    placing = (positions[:, None] % tile_rows == jnp.arange(tile_rows)[None, :]).astype(
        jnp.float32
    ) * active[:, None]
    placed = jnp.einsum("st,sjf->tjf", placing, product, precision=HIGHEST)
    return placed.reshape(tile_rows * tile_size, feature_width)


def cycle_forward(block_data, tile_values, tile_pos, tile_counts):
    blocks = lax.axis_size("blk")
    half_cycle = blocks // 2
    own_block = lax.axis_index("blk")
    replica = lax.axis_index("rep")
    first_section = replica * half_cycle
    current = jnp.where(replica == 0, block_data, half_turn(block_data))

    def contribute(section_number, held_block):
        column = (own_block - first_section - section_number) % blocks
        values, positions, live_count = pick_pair(tile_values, tile_pos, tile_counts, column)
        return pair_rows(values, positions, live_count, held_block)

    running_sum = contribute(0, current)

    def advance(section_number, loop_state):
        partial_value, held_block = loop_state
        held_block = shift_one(held_block)
        return (partial_value + contribute(section_number, held_block), held_block)

    running_sum, current = lax.fori_loop(1, half_cycle, advance, (running_sum, current))
    return replica_total(running_sum)


def cycle_backward(gradients, tile_values, tile_pos, tile_counts):
    blocks = lax.axis_size("blk")
    half_cycle = blocks // 2
    own_block = lax.axis_index("blk")
    replica = lax.axis_index("rep")
    first_section = replica * half_cycle
    zero_sum = jnp.zeros(gradients.shape, jnp.float32)

    def advance(section_number, held_block):
        column = (own_block - first_section - section_number) % blocks
        values, positions, live_count = pick_pair(tile_values, tile_pos, tile_counts, column)
        return shift_one(held_block + pair_columns(values, positions, live_count, gradients))

    held_block = lax.fori_loop(0, half_cycle, advance, zero_sum)
    held_block = jnp.where(replica == 0, half_turn(held_block), held_block)
    return replica_total(held_block)


def body(features, weight, tile_values, tile_pos, tile_counts, out_grad):
    node_count = features.shape[0] * lax.axis_size("blk")
    aggregated = cycle_forward(features, tile_values, tile_pos, tile_counts)
    pre_act = jnp.dot(aggregated, weight, precision=HIGHEST)
    gate_value = jax.nn.sigmoid(pre_act)
    output = pre_act * gate_value
    pre_grad = out_grad * gate_value * (1.0 + pre_act * (1.0 - gate_value))
    weight_grad = weight_total(aggregated, pre_grad, node_count)
    agg_grad = jnp.dot(pre_grad, weight.T, precision=HIGHEST)
    feature_grad = cycle_backward(agg_grad, tile_values, tile_pos, tile_counts)
    return (output, feature_grad, weight_grad)


def solution(mesh):
    return jax.shard_map(
        body,
        mesh=mesh,
        in_specs=(
            P("blk", None),
            P(),
            P("blk", None, None, None, None),
            P("blk", None, None),
            P("blk", None),
            P("blk", None),
        ),
        out_specs=(P("blk", None), P("blk", None), P()),
        check_vma=False,
    )
```

profile of v0, /device:TPU:1, one launch (start us, length us, event | category | flops | bytes accessed | tf_op | source)
XLA Modules:
  0.0 1340.0 jit_solution(1323528377522211957)
XLA Ops:
  18.2 343.1 %while.34 = (s32[]{:T(128)}, f32[256,128]{1,0:T(8,128)S(1)}, f32[256,128]{1,0:T(8,128)S(1)}, s32[]{:T(128)}, s32[1,64,3]{2,1,0:T(8,128)S(1)}, /*index=5*/s32[1,6...) while((s32[]{:T(128)}, f32[256,128]{1,0:T(8,128)S(1)}, ...), condition=%wide.region_1.3_spmd, body=%wide.region_0.2_spmd.sunk | while | flops 76760176 | bytes 2757062 | solution.py:92
  362.0 31.6 %all-reduce.4.cloned.1.call-done = f32[256,128]{1,0:T(8,128)} async-done(((f32[256,128]{1,0:T(8,128)}), f32[256,128]{1,0:T(8,128)}) %all-reduce.4.cloned.1.call-update) | async-done | bytes 131088 | tf_op jit(solution)/shard_map/psum | solution.py:25
  396.1 420.4 %while.35 = (s32[]{:T(128)}, f32[256,128]{1,0:T(8,128)S(1)}, s32[]{:T(128)}, s32[1,64,3]{2,1,0:T(8,128)S(1)}, s32[1,64]{1,0:T(1,128)}, /*index=5*/f32[1,64,3,128...) while((s32[]{:T(128)}, f32[256,128]{1,0:T(8,128)S(1)}, ...), condition=%wide.region_4.6_spmd, body=%wide.region_3.5_spmd.sunk | while | flops 76760192 | bytes 2494934 | solution.py:109
  420.9 8.6 collective-permute-done.1
  434.3 8.6 collective-permute-done.1
  461.0 8.6 collective-permute-done.1
  474.3 8.6 collective-permute-done.1
  501.0 8.6 collective-permute-done.1
  514.3 8.6 collective-permute-done.1
  527.7 8.6 collective-permute-done.1
  554.4 8.6 collective-permute-done.1
  567.7 8.6 collective-permute-done.1
  594.4 8.6 collective-permute-done.1
  607.8 8.6 collective-permute-done.1
  621.1 8.6 collective-permute-done.1
  647.8 8.6 collective-permute-done.1
  661.1 8.6 collective-permute-done.1
  687.8 8.6 collective-permute-done.1
  701.2 8.6 collective-permute-done.1
  741.2 8.6 collective-permute-done.1
  781.2 8.6 collective-permute-done.1
  794.6 8.6 collective-permute-done.1
  822.5 478.3 %all-reduce.8.cloned.1.call-done = f32[128,256]{1,0:T(8,128)} async-done(((f32[128,256]{1,0:T(8,128)}), f32[128,256]{1,0:T(8,128)}) %all-reduce.8.cloned.1.call-update) | async-done | bytes 131088 | tf_op jit(solution)/shard_map/psum | solution.py:30
  1302.4 29.5 %all-reduce.6.cloned.1.call-done = f32[256,128]{1,0:T(8,128)} async-done(((f32[256,128]{1,0:T(8,128)}), f32[256,128]{1,0:T(8,128)}) %all-reduce.6.cloned.1.call-update) | async-done | bytes 131088 | tf_op jit(solution)/shard_map/psum | solution.py:25
  (805 shorter events, 617.6 us)
Async XLA Ops:
  7.2 386.4 %all-reduce.4.cloned.1.call-start = ((), (), s32[]{:S(2)}) async-start(), calls=%async_computation | async-start | bytes 262144 | tf_op jit(solution)/shard_map/psum | solution.py:25
  56.6 8.7 collective-permute-start
  67.9 8.7 collective-permute-start
  101.8 8.7 collective-permute-start
  146.9 8.7 collective-permute-start
  192.0 8.7 collective-permute-start
  237.1 8.7 collective-permute-start
  282.3 8.7 collective-permute-start
  327.4 8.7 collective-permute-start
  361.9 938.9 %all-reduce.8.cloned.1.call-start = ((), (), s32[]{:S(2)}) async-start(), calls=%async_computation.2 | async-start | bytes 262144 | tf_op jit(solution)/shard_map/psum | solution.py:30
  420.8 8.7 collective-permute-start.1
  460.9 8.7 collective-permute-start.1
  500.9 8.7 collective-permute-start.1
  514.3 8.7 collective-permute-start.1
  554.3 8.7 collective-permute-start.1
  594.3 8.7 collective-permute-start.1
  607.7 8.7 collective-permute-start.1
  647.7 8.7 collective-permute-start.1
  687.7 8.7 collective-permute-start.1
  701.1 8.7 collective-permute-start.1
  741.1 8.7 collective-permute-start.1
  781.2 8.7 collective-permute-start.1
  794.5 8.7 collective-permute-start.1
  817.6 514.3 %all-reduce.6.cloned.1.call-start = ((), (), s32[]{:S(2)}) async-start(), calls=%async_computation.1 | async-start | bytes 262144 | tf_op jit(solution)/shard_map/psum | solution.py:25
  (48 other events, 1560.5 us)
Sparse Core Ops, SparseCore 0:
  362.0 31.4 all-reduce.3
  817.7 483.0 all-reduce.7
  1304.0 27.9 all-reduce.5
where the time goes:
time: 1340 us
  waiting for transfers between devices  1000 us (75%)
  matrix products  132 us (10%)
  local copies, waits for them, and re-layouts  120 us (9%)
  other arithmetic  48.5 us (4%)
  starting transfers between devices  17.4 us (1%)
  between operations  13.9 us (1%)
    psum x1, waiting for transfers between devices, weight_total(): return lax.psum(partial_value, 'blk') / math.sqrt(node_count)  478 us
    ppermute x65, waiting for transfers between devices, passed_along(): return lax.ppermute(x, axis, [(i, (i + by) % count) for i in range(count)])  463 us
    dynamic_slice x64, local copies, waits for them, and re-layouts, pick_pair(): lax.dynamic_index_in_dim(tile_counts[0], column, 0, keepdims=False)  79.5 us
    psum x2, waiting for transfers between devices, replica_total(): return lax.psum(partial_value, 'rep')  61.1 us
    dot_general x32, matrix products, pair_columns(): product = jnp.einsum('sij,sif->sjf', values, picked, precision=HIGHEST)  46.3 us
    dot_general x32, matrix products, pair_rows(): product = jnp.einsum('sij,sjf->sif', values, picked, precision=HIGHEST)  41.9 us
  transfers between devices with their start and end apart: 68, of which 66 were waited for; matrix products, arithmetic and copies ran while one was open for 5% of the time, Pallas kernels for 0%

commit v1 on v0

v1 whole, which is shorter than its diff:
```python
import math

import jax
import jax.numpy as jnp
from jax import lax
from jax.experimental import pallas as pl
from jax.experimental.pallas import tpu as pltpu
from jax.sharding import PartitionSpec as P

HIGHEST = lax.Precision.HIGHEST
MESH = pl.DeviceIdType.MESH
F32, BF16 = jnp.float32, jnp.bfloat16
NODES = 16384
TILE = 128


def split(x):
    hi = x.astype(BF16)
    return hi, (x - hi.astype(F32)).astype(BF16)


def kernel(
    feat_hbm, weight_hbm, tiles_hbm, pos, counts, ograd_hbm,
    out_hbm, fgrad_hbm, wgrad_hbm,
    tv, ah, al, feat, wside, acc, swap, agg_t, wt, og, pgrad, gs, outv,
    part, sibq, b_opp, b_full, a_opp, a_full, xr, fgv,
    wg, wr1, wr2, fin, wr3, wgv,
    tile_sem, load_sem, first_sem, store_sem,
    f_send, f_recv, fs_send, fs_recv, x_send, x_recv, swap_send, swap_recv,
    q_send, q_recv, bo_send, bo_recv, bf_send, bf_recv, ao_send, ao_recv, af_send, af_recv,
    t_send, t_recv, w1_send, w1_recv, w2_send, w2_recv, w3_send, w3_recv,
):
    blk, rep = lax.axis_index("blk"), lax.axis_index("rep")
    y, z = lax.rem(lax.div(blk, 16), 4), lax.rem(lax.div(blk, 4), 4)
    xl, k = lax.rem(lax.div(blk, 2), 2), lax.rem(blk, 2)
    native = xl == rep

    def at(yy, zz, xx, kk):
        return ((lax.rem(yy + 8, 4) * 4 + lax.rem(zz + 8, 4)) * 2 + xx) * 2 + kk

    def near(da, db):
        return (at(y + da * (1 - k) + db * k, z + da * k + db * (1 - k), xl, k), rep)

    sibling = (at(y, z, xl, 1 - k), rep)

    def remote(src, dst, ssem, rsem, dev):
        return pltpu.make_async_remote_copy(
            src_ref=src, dst_ref=dst, send_sem=ssem, recv_sem=rsem, device_id=dev, device_id_type=MESH
        )

    def arrived(dst, rsem):
        remote(dst, dst, rsem, rsem, sibling).wait_recv()

    def sent(src, ssem):
        remote(src, src, ssem, ssem, sibling).wait_send()

    tile_copy = pltpu.make_async_copy(tiles_hbm.at[:, rep], tv, tile_sem)
    tile_copy.start()
    loads = [
        pltpu.make_async_copy(weight_hbm, wt, load_sem.at[0]),
        pltpu.make_async_copy(ograd_hbm, og, load_sem.at[1]),
    ]
    for c in loads:
        c.start()

    barrier = pltpu.get_barrier_semaphore()
    plane_peers = [(dy, dz) for dy in range(4) for dz in range(4) if (dy, dz) != (0, 0)]
    line_peers = [(i, j, l) for i in range(2) for j in range(2) for l in range(2) if (i, j, l) != (0, 0, 0)]

    def plane_dev(dy, dz):
        return (at(y + dy, z + dz, xl, k), rep)

    def line_dev(i, j, l):
        return (at(y, z, lax.rem(xl + j, 2), lax.rem(k + l, 2)), lax.rem(rep + i, 2))

    for d in plane_peers:
        pl.semaphore_signal(barrier, inc=1, device_id=plane_dev(*d), device_id_type=MESH)
    for d in line_peers:
        pl.semaphore_signal(barrier, inc=1, device_id=line_dev(*d), device_id_type=MESH)
    pl.semaphore_wait(barrier, len(plane_peers) + len(line_peers))

    half = lax.rem(xl + rep, 2)
    remote(
        feat_hbm.at[half], feat.at[0, half], x_send, x_recv.at[half], (at(y, z, 1 - xl, k), xl)
    ).start()

    @pl.when(native)
    def _():
        c = pltpu.make_async_copy(feat_hbm, feat.at[0, pl.ds(0, 2)], first_sem)
        c.start()
        c.wait()

    @pl.when(jnp.logical_not(native))
    def _():
        for h in range(2):
            arrived(feat.at[0, h], x_recv.at[h])

    def spot(da, db, h):
        return (da % 4 * 4 + db % 4) * 2 + h

    def send_f(da, db, h, ma, mb):
        there = spot(da - ma, db - mb, h)
        remote(
            feat.at[0, spot(da, db, h)], feat.at[0, there], f_send, f_recv.at[there], near(ma, mb)
        ).start()

    def wait_f(da, db, h):
        i = spot(da, db, h)
        arrived(feat.at[0, i], f_recv.at[i])

    def give_f(da, db):
        i = spot(da, db, 0)
        remote(
            feat.at[0, pl.ds(i, 2)], feat.at[1, pl.ds(i, 2)], fs_send, fs_recv.at[i // 2], sibling
        ).start()

    def prep(kk, da):
        def one(db, carry):
            if kk == 0:
                own = k
            else:
                own = 1 - k
            yy = lax.rem(y + da * (1 - own) + db * own, 4)
            zz = lax.rem(z + da * own + db * (1 - own), 4)
            c = ((yy * 4 + zz) * 2 + rep) * 2 + own
            base = yy * 4 + zz
            n = counts[0, c]
            p = [pos[0, c, s] for s in range(3)]
            for q in range(4):
                s = jnp.where(p[0] == q, 0, jnp.where(p[1] == q, 1, 2))
                live = ((p[0] == q) & (n > 0)) | ((p[1] == q) & (n > 1)) | ((p[2] == q) & (n > 2))
                t = tv[base, own, s] * jnp.where(live, 1.0, 0.0).astype(F32)
                hi, lo = split(t)
                col = pl.multiple_of((kk * 16 + da * 4 + db) * 256 + q % 2 * TILE, TILE)
                rows = slice(q // 2 * TILE, (q // 2 + 1) * TILE)
                ah[rows, pl.ds(col, TILE)] = hi
                al[rows, pl.ds(col, TILE)] = lo
            return carry

        lax.fori_loop(0, 4, one, 0)

    def multiply(kk, da):
        hi, lo = split(feat[kk, da * 8 : da * 8 + 8].reshape(1024, TILE))
        wside[:, 0:TILE] = hi
        wside[:, TILE : 2 * TILE] = lo
        cols = slice((kk * 16 + da * 4) * 256, (kk * 16 + da * 4 + 4) * 256)
        w = wside[...]
        acc[...] += jnp.dot(ah[:, cols], w, preferred_element_type=F32) + jnp.dot(
            al[:, cols], w, preferred_element_type=F32
        )

    def sib_group(da):
        for db in range(4):
            i = da * 4 + db
            arrived(feat.at[1, pl.ds(2 * i, 2)], fs_recv.at[i])

    for h in range(2):
        send_f(0, 0, h, 1, 0)
        send_f(0, 0, 1 - h, -1, 0)
    for h in range(2):
        send_f(0, 0, h, 0, 1)
        send_f(0, 0, 1 - h, 0, -1)
    give_f(0, 0)
    acc[...] = jnp.zeros_like(acc)
    tile_copy.wait()
    prep(0, 0)
    wait_f(3, 0, 0)
    send_f(3, 0, 0, 1, 0)
    wait_f(1, 0, 1)
    send_f(1, 0, 1, -1, 0)
    wait_f(3, 0, 1)
    wait_f(1, 0, 0)
    for da in (3, 1):
        give_f(da, 0)
    for h in range(2):
        for da in (3, 1):
            send_f(da, 0, h, 0, 1)
            send_f(da, 0, 1 - h, 0, -1)
    prep(1, 0)
    wait_f(0, 3, 0)
    send_f(0, 3, 0, 0, 1)
    wait_f(0, 1, 1)
    send_f(0, 1, 1, 0, -1)
    wait_f(2, 0, 0)
    wait_f(2, 0, 1)
    give_f(2, 0)
    for h in range(2):
        send_f(2, 0, h, 0, 1)
        send_f(2, 0, 1 - h, 0, -1)
    wait_f(0, 3, 1)
    give_f(0, 3)
    wait_f(0, 1, 0)
    give_f(0, 1)
    prep(0, 3)
    for da in (3, 1, 2):
        wait_f(da, 3, 0)
        send_f(da, 3, 0, 0, 1)
        wait_f(da, 1, 1)
        send_f(da, 1, 1, 0, -1)
        wait_f(da, 3, 1)
        give_f(da, 3)
        wait_f(da, 1, 0)
        give_f(da, 1)
        before = {3: 0, 1: 3, 2: 1}[da]
        wait_f(before, 2, 0)
        wait_f(before, 2, 1)
        give_f(before, 2)
        if da == 3:
            prep(1, 3)
            prep(0, 1)
        if da == 1:
            prep(1, 1)
            prep(0, 2)
            prep(1, 2)
        multiply(0, before)
        sib_group(before)
        multiply(1, before)
    wait_f(2, 2, 0)
    wait_f(2, 2, 1)
    give_f(2, 2)
    multiply(0, 2)
    sib_group(2)
    multiply(1, 2)

    swap[0] = acc[:, 0:TILE] + acc[:, TILE : 2 * TILE]
    twin = (blk, 1 - rep)
    c = remote(swap.at[0], swap.at[1], swap_send, swap_recv, twin)
    c.start()
    for l in loads:
        l.wait()
    c.wait_recv()
    agg = swap[0] + swap[1]
    w = wt[...]
    pre = jnp.dot(agg, w, precision=HIGHEST, preferred_element_type=F32)
    gate = jax.nn.sigmoid(pre)
    outv[...] = pre * gate
    pg = og[...] * gate * (1.0 + pre * (1.0 - gate))
    pgrad[...] = pg
    g_t = lax.dot_general(w, pg, (((1,), (1,)), ((), ())), precision=HIGHEST, preferred_element_type=F32)
    hi, lo = split(g_t)
    gs[0:TILE] = hi
    gs[TILE : 2 * TILE] = lo
    out_copy = pltpu.make_async_copy(outv, out_hbm, store_sem.at[0])
    out_copy.start()

    def back(kk, da):
        cols = slice((kk * 16 + da * 4) * 256, (kk * 16 + da * 4 + 4) * 256)
        main = jnp.dot(gs[...], ah[:, cols], preferred_element_type=F32)
        rest = jnp.dot(gs[0:TILE], al[:, cols], preferred_element_type=F32)
        total = main[0:TILE] + main[TILE : 2 * TILE] + rest
        for db in range(4):
            for h in range(2):
                part[kk, spot(da, db, h)] = total[h * 64 : h * 64 + 64, db * 256 : db * 256 + 256]

    def give_q(da):
        for db in (2, 1, 3, 0):
            i = spot(da, db, 0)
            remote(
                part.at[1, pl.ds(i, 2)], sibq.at[pl.ds(i, 2)], q_send, q_recv.at[i // 2], sibling
            ).start()

    def take_q(da, db):
        i = spot(da, db, 0)
        arrived(sibq.at[pl.ds(i, 2)], q_recv.at[i // 2])
        part[0, i : i + 2] = part[0, i : i + 2] + sibq[i : i + 2]

    def step1(da):
        take_q(da, 2)
        for h, m in ((0, 1), (1, -1)):
            remote(
                part.at[0, spot(da, 2, h)], b_opp.at[da, h], bo_send, bo_recv.at[da, h], near(0, m)
            ).start()

    def send_full(da, db, h, n, m):
        remote(
            part.at[0, spot(da, db, h)], b_full.at[da, n, h], bf_send, bf_recv.at[da, n, h], near(0, m)
        ).start()

    def step2(da):
        take_q(da, 1)
        send_full(da, 1, 1, 0, 1)
        take_q(da, 3)
        send_full(da, 3, 0, 1, -1)
        for db, h, m in ((1, 0, 1), (3, 1, -1)):
            arrived(b_opp.at[da, h], bo_recv.at[da, h])
            i = spot(da, db, h)
            part[0, i] = part[0, i] + b_opp[da, h]
            send_full(da, db, h, h, m)

    def step3(da):
        take_q(da, 0)
        for n in range(2):
            for h in range(2):
                arrived(b_full.at[da, n, h], bf_recv.at[da, n, h])
        i = spot(da, 0, 0)
        part[0, i : i + 2] = part[0, i : i + 2] + (b_full[da, 0] + b_full[da, 1])

    def send_a(da, h, n, m):
        remote(
            part.at[0, spot(da, 0, h)], a_full.at[n, h], af_send, af_recv.at[n, h], near(m, 0)
        ).start()

    def weight_term():
        agg_t[...] = (swap[0] + swap[1]).T
        rows = agg_t[pl.ds(pl.multiple_of(rep * 64, 64), 64), :]
        term = jnp.dot(rows, pgrad[...], precision=HIGHEST, preferred_element_type=F32)
        for i in range(8):
            for j in range(2):
                wg[i * 2 + j] = term[i * 8 : i * 8 + 8, j * TILE : j * TILE + TILE]
        for dy, dz in plane_peers:
            there = lax.rem(y + dy, 4) * 4 + lax.rem(z + dz, 4)
            remote(wg.at[there], wr1.at[dy * 4 + dz - 1], w1_send, w1_recv, plane_dev(dy, dz)).start()

    here = y * 4 + z
    line = (rep * 2 + xl) * 2 + k

    def weight_line():
        arrived(wr1, w1_recv)
        total = wg[here]
        for i in range(15):
            total = total + wr1[i]
        wr2[line] = total
        for d in line_peers:
            remote(wr2.at[line], wr2.at[line], w2_send, w2_recv, line_dev(*d)).start()

    def weight_plane():
        arrived(wr2.at[pl.ds(0, 7)], w2_recv)
        for i in range(2):
            total = (wr2[4 * i] + wr2[4 * i + 1]) + (wr2[4 * i + 2] + wr2[4 * i + 3])
            wr3[here, i] = total * (1.0 / math.sqrt(NODES))
        for d in plane_peers:
            remote(wr3.at[here], wr3.at[here], w3_send, w3_recv, plane_dev(*d)).start()

    back(1, 2)
    give_q(2)
    back(0, 2)
    step1(2)
    back(1, 1)
    give_q(1)
    step2(2)
    back(0, 1)
    step1(1)
    back(1, 3)
    give_q(3)
    step2(1)
    back(0, 3)
    step1(3)
    back(1, 0)
    give_q(0)
    step2(3)
    back(0, 0)
    step1(0)
    step2(0)
    weight_term()
    step3(2)
    for h, m in ((0, 1), (1, -1)):
        remote(part.at[0, spot(2, 0, h)], a_opp.at[h], ao_send, ao_recv.at[h], near(m, 0)).start()
    step3(1)
    send_a(1, 1, 0, 1)
    weight_line()
    step3(3)
    send_a(3, 0, 1, -1)
    for da, h, m in ((1, 0, 1), (3, 1, -1)):
        arrived(a_opp.at[h], ao_recv.at[h])
        i = spot(da, 0, h)
        part[0, i] = part[0, i] + a_opp[h]
        send_a(da, h, h, m)
    weight_plane()
    step3(0)
    for n in range(2):
        for h in range(2):
            arrived(a_full.at[n, h], af_recv.at[n, h])
    part[0, 0:2] = part[0, 0:2] + (a_full[0] + a_full[1])

    total = part.at[0, pl.ds(0, 2)]

    @pl.when(native)
    def _():
        remote(total, xr.at[1], t_send.at[0], t_recv.at[1], (at(y, z, xl, k), 1 - rep)).start()
        arrived(xr.at[0], t_recv.at[0])
        fgv[...] = (part[0, 0:2] + xr[0]).reshape(TILE, 256).T
        sent(total, t_send.at[0])

    @pl.when(jnp.logical_not(native))
    def _():
        remote(total, xr.at[0], t_send.at[0], t_recv.at[0], (at(y, z, 1 - xl, k), rep)).start()
        remote(total, xr.at[0], t_send.at[1], t_recv.at[0], (at(y, z, 1 - xl, k), 1 - rep)).start()
        arrived(xr.at[0], t_recv.at[0])
        arrived(xr.at[1], t_recv.at[1])
        fgv[...] = (xr[0] + xr[1]).reshape(TILE, 256).T
        sent(total, t_send.at[0])
        sent(total, t_send.at[1])

    fg_copy = pltpu.make_async_copy(fgv, fgrad_hbm, store_sem.at[1])
    fg_copy.start()

    arrived(wr3.at[pl.ds(0, 15)], w3_recv)
    for half_index in range(2):
        for i in range(8):
            for j in range(2):
                wgv[half_index * 64 + i * 8 : half_index * 64 + i * 8 + 8, j * TILE : j * TILE + TILE] = wr3[
                    i * 2 + j, half_index
                ]
    wg_copy = pltpu.make_async_copy(wgv, wgrad_hbm, store_sem.at[2])
    wg_copy.start()

    sent(feat.at[0, half], x_send)
    sent(feat.at[0, pl.ds(0, 30)], f_send)
    sent(feat.at[0], fs_send)
    sent(swap.at[0], swap_send)
    sent(part.at[1], q_send)
    sent(b_opp, bo_send)
    sent(b_full, bf_send)
    sent(a_opp, ao_send)
    sent(a_full, af_send)
    sent(wr1, w1_send)
    sent(wr2.at[pl.ds(0, 7)], w2_send)
    sent(wr3.at[pl.ds(0, 15)], w3_send)
    out_copy.wait()
    fg_copy.wait()
    wg_copy.wait()


def body(features, weight, tile_values, tile_pos, tile_counts, out_grad):
    dma = pltpu.SemaphoreType.DMA
    vm = pltpu.VMEM
    any_space = pl.BlockSpec(memory_space=pl.ANY)
    smem = pl.BlockSpec(memory_space=pltpu.SMEM)
    return pl.pallas_call(
        kernel,
        out_shape=(
            jax.ShapeDtypeStruct((256, 256), F32),
            jax.ShapeDtypeStruct((256, 128), F32),
            jax.ShapeDtypeStruct((128, 256), F32),
        ),
        in_specs=[any_space, any_space, any_space, smem, smem, any_space],
        out_specs=(any_space, any_space, any_space),
        scratch_shapes=[
            vm((16, 2, 3, TILE, TILE), F32),
            vm((256, 8192), BF16),
            vm((256, 8192), BF16),
            vm((2, 32, TILE, TILE), F32),
            vm((1024, 256), BF16),
            vm((256, 256), F32),
            vm((2, 256, TILE), F32),
            vm((TILE, 256), F32),
            vm((TILE, 256), F32),
            vm((256, 256), F32),
            vm((256, 256), F32),
            vm((256, 256), BF16),
            vm((256, 256), F32),
            vm((2, 32, 64, 256), F32),
            vm((32, 64, 256), F32),
            vm((4, 2, 64, 256), F32),
            vm((4, 2, 2, 64, 256), F32),
            vm((2, 64, 256), F32),
            vm((2, 2, 64, 256), F32),
            vm((2, 2, 64, 256), F32),
            vm((256, TILE), F32),
            vm((16, 8, TILE), F32),
            vm((15, 8, TILE), F32),
            vm((8, 8, TILE), F32),
            vm((8, TILE), F32),
            vm((16, 2, 8, TILE), F32),
            vm((TILE, 256), F32),
            dma, dma((2,)), dma, dma((3,)),
            dma, dma((32,)), dma, dma((16,)), dma, dma((2,)), dma, dma,
            dma, dma((16,)), dma, dma((4, 2)), dma, dma((4, 2, 2)), dma, dma((2,)), dma, dma((2, 2)),
            dma((2,)), dma((2,)), dma, dma, dma, dma, dma, dma,
        ],
        compiler_params=pltpu.CompilerParams(
            collective_id=0, has_side_effects=True, vmem_limit_bytes=48 * 1024 * 1024
        ),
        cost_estimate=pl.CostEstimate(flops=3_000_000_000, bytes_accessed=8_000_000, transcendentals=65536),
    )(
        features.reshape(2, TILE, TILE),
        weight,
        tile_values.reshape(16, 2, 2, 3, TILE, TILE),
        tile_pos,
        tile_counts,
        out_grad,
    )


def solution(mesh):
    return jax.shard_map(
        body,
        mesh=mesh,
        in_specs=(
            P("blk", None),
            P(),
            P("blk", None, None, None, None),
            P("blk", None, None),
            P("blk", None),
            P("blk", None),
        ),
        out_specs=(P("blk", None), P("blk", None), P()),
        check_vma=False,
    )
```

time: 1340 us -> 84.6 us (0.06)
  the two profiles are of different devices: /device:TPU:1 before, /device:TPU:2 now
where the time goes in v1:
time: 84.6 us; the launch traced here: 84.4 us
  Pallas kernels  77.5 us (92%)
  local copies, waits for them, and re-layouts  6.2 us (7%)
    pallas_call x1, Pallas kernels, body(): pl.pallas_call(kernel, out_shape=(jax.ShapeDtypeStruct((256, 256), F32),...  77.5 us
    unnamed x12, local copies, waits for them, and re-layouts  6.2 us

profile of v1, /device:TPU:2, one launch (start us, length us, event | category | flops | bytes accessed | tf_op | source)
XLA Modules:
  0.0 84.4 jit_solution(12692640915483235410)
XLA Ops:
  0.6 0.8 copy.9.pos
  1.4 0.0 copy-start
  1.4 0.9 %copy-done = f32[256,256]{1,0:T(8,128)S(1)} copy-done((f32[256,256]{1,0:T(8,128)S(1)}, f32[256,256]{1,0:T(8,128)}, u32[]{:S(2)}) %copy-start) | copy-done | bytes 262168
  2.4 0.0 copy-start.1
  2.4 0.9 %copy-done.1 = f32[256,128]{1,0:T(8,128)S(1)} copy-done((f32[256,128]{1,0:T(8,128)S(1)}, f32[256,128]{1,0:T(8,128)}, u32[]{:S(2)}) %copy-start.1) | copy-done | bytes 131096
  3.3 0.0 copy-start.2
  3.3 0.9 %copy-done.2 = f32[128,256]{1,0:T(8,128)S(1)} copy-done((f32[128,256]{1,0:T(8,128)S(1)}, f32[128,256]{1,0:T(8,128)}, u32[]{:S(2)}) %copy-start.2) | copy-done | bytes 131096
  4.2 0.0 copy-start.3
  4.2 0.7 copy-done.3
  4.8 77.5 %shard_map.85 = (f32[256,256]{1,0:T(8,128)S(1)}, f32[256,128]{1,0:T(8,128)S(1)}, f32[128,256]{1,0:T(8,128)S(1)}) custom-call(f32[2,128,128]{2,1,0:T(8,128)S(1)} %bitcast.2, f32[128,256]{1,0:T(8,128)S(1)} %copy-done.2, f32[16,2,2,3,128,128]{5,4,3,2,1,0:T(8,128)} %bitcast.3, s32[1,64,3]{2,1,0:T(8,128)S(1)} %copy.9.pos, s32[1,64]{1,0:T(1,128)S(1)} %copy-done.3, ...), custom_call_target="tpu_custom_call" | custom-call | flops 3000000000 | bytes 8000000 | tf_op jit(solution)/shard_map/pallas_call | solution.py:429
  82.3 0.7 copy.13
  83.0 0.7 copy.14
  83.7 0.7 copy.15
Async XLA Ops:
  1.4 0.9 %copy-start = (f32[256,256]{1,0:T(8,128)S(1)}, f32[256,256]{1,0:T(8,128)}, u32[]{:S(2)}) copy-start(f32[256,256]{1,0:T(8,128)} %ograd_hbm.1) | copy-start | bytes 786436
  2.4 0.9 %copy-start.1 = (f32[256,128]{1,0:T(8,128)S(1)}, f32[256,128]{1,0:T(8,128)}, u32[]{:S(2)}) copy-start(f32[256,128]{1,0:T(8,128)} %param.6) | copy-start | bytes 393220
  3.3 0.9 %copy-start.2 = (f32[128,256]{1,0:T(8,128)S(1)}, f32[128,256]{1,0:T(8,128)}, u32[]{:S(2)}) copy-start(f32[128,256]{1,0:T(8,128)} %weight_hbm.1) | copy-start | bytes 393220
  4.2 0.7 copy-start.3

commit v2 on v1

--- a/solution.py
+++ b/solution.py
@@ -23,17 +23,17 @@
     feat_hbm, weight_hbm, tiles_hbm, pos, counts, ograd_hbm,
     out_hbm, fgrad_hbm, wgrad_hbm,
     tv, ah, al, feat, wside, acc, swap, agg_t, wt, og, pgrad, gs, outv,
-    part, sibq, b_opp, b_full, a_opp, a_full, xr, fgv,
-    wg, wr1, wr2, fin, wr3, wgv,
+    part, sibq, b_opp, b_full, a_full, xr, fgv,
+    wg, wr1, wr2, wr3, wgv,
     tile_sem, load_sem, first_sem, store_sem,
-    f_send, f_recv, fs_send, fs_recv, x_send, x_recv, swap_send, swap_recv,
-    q_send, q_recv, bo_send, bo_recv, bf_send, bf_recv, ao_send, ao_recv, af_send, af_recv,
+    f_send, f_recv, fs_send, fs_recv, x_send, n_send, swap_send, swap_recv,
+    q_send, q_recv, bo_send, bo_recv, bf_send, bf_recv, af_send, af_recv,
     t_send, t_recv, w1_send, w1_recv, w2_send, w2_recv, w3_send, w3_recv,
 ):
     blk, rep = lax.axis_index("blk"), lax.axis_index("rep")
     y, z = lax.rem(lax.div(blk, 16), 4), lax.rem(lax.div(blk, 4), 4)
     xl, k = lax.rem(lax.div(blk, 2), 2), lax.rem(blk, 2)
-    native = xl == rep
+    native = k == rep
 
     def at(yy, zz, xx, kk):
         return ((lax.rem(yy + 8, 4) * 4 + lax.rem(zz + 8, 4)) * 2 + xx) * 2 + kk
@@ -54,7 +54,7 @@
     def sent(src, ssem):
         remote(src, src, ssem, ssem, sibling).wait_send()
 
-    tile_copy = pltpu.make_async_copy(tiles_hbm.at[:, rep], tv, tile_sem)
+    tile_copy = pltpu.make_async_copy(tiles_hbm.at[:, :, rep], tv, tile_sem)
     tile_copy.start()
     loads = [
         pltpu.make_async_copy(weight_hbm, wt, load_sem.at[0]),
@@ -73,27 +73,30 @@
     def line_dev(i, j, l):
         return (at(y, z, lax.rem(xl + j, 2), lax.rem(k + l, 2)), lax.rem(rep + i, 2))
 
-    for d in plane_peers:
-        pl.semaphore_signal(barrier, inc=1, device_id=plane_dev(*d), device_id_type=MESH)
-    for d in line_peers:
-        pl.semaphore_signal(barrier, inc=1, device_id=line_dev(*d), device_id_type=MESH)
-    pl.semaphore_wait(barrier, len(plane_peers) + len(line_peers))
-
-    half = lax.rem(xl + rep, 2)
-    remote(
-        feat_hbm.at[half], feat.at[0, half], x_send, x_recv.at[half], (at(y, z, 1 - xl, k), xl)
-    ).start()
-
-    @pl.when(native)
-    def _():
-        c = pltpu.make_async_copy(feat_hbm, feat.at[0, pl.ds(0, 2)], first_sem)
-        c.start()
-        c.wait()
+    def over(m):
+        return (at(y + m * k, z + m * (1 - k), 1 - xl, 1 - k), k)
+
+    def over_from(m, i):
+        return (at(y + m * (1 - k), z + m * k, 1 - xl, 1 - k), i)
+
+    def greet(dev):
+        pl.semaphore_signal(barrier, inc=1, device_id=dev, device_id_type=MESH)
+
+    twin = (blk, 1 - rep)
+    peers = [near(1, 0), near(-1, 0), near(2, 0), near(0, 1), near(0, -1), sibling, twin]
+    for d in peers:
+        greet(d)
+
+    for i in range(2):
+        greet((at(y, z, 1 - xl, 1 - k), i))
 
     @pl.when(jnp.logical_not(native))
     def _():
-        for h in range(2):
-            arrived(feat.at[0, h], x_recv.at[h])
+        for m in (1, -1, 2):
+            for i in range(2):
+                greet(over_from(m, i))
+
+    pl.semaphore_wait(barrier, len(peers) + 2 + 3)
 
     def spot(da, db, h):
         return (da % 4 * 4 + db % 4) * 2 + h
@@ -122,14 +125,15 @@
                 own = 1 - k
             yy = lax.rem(y + da * (1 - own) + db * own, 4)
             zz = lax.rem(z + da * own + db * (1 - own), 4)
-            c = ((yy * 4 + zz) * 2 + rep) * 2 + own
+            xx = lax.rem(xl + own + rep, 2)
             base = yy * 4 + zz
+            c = (base * 2 + xx) * 2 + rep
             n = counts[0, c]
-            p = [pos[0, c, s] for s in range(3)]
+            p = [pos[s, 0, c] for s in range(3)]
             for q in range(4):
                 s = jnp.where(p[0] == q, 0, jnp.where(p[1] == q, 1, 2))
                 live = ((p[0] == q) & (n > 0)) | ((p[1] == q) & (n > 1)) | ((p[2] == q) & (n > 2))
-                t = tv[base, own, s] * jnp.where(live, 1.0, 0.0).astype(F32)
+                t = tv[base, xx, s] * jnp.where(live, 1.0, 0.0).astype(F32)
                 hi, lo = split(t)
                 col = pl.multiple_of((kk * 16 + da * 4 + db) * 256 + q % 2 * TILE, TILE)
                 rows = slice(q // 2 * TILE, (q // 2 + 1) * TILE)
@@ -154,9 +158,26 @@
             i = da * 4 + db
             arrived(feat.at[1, pl.ds(2 * i, 2)], fs_recv.at[i])
 
-    for h in range(2):
-        send_f(0, 0, h, 1, 0)
-        send_f(0, 0, 1 - h, -1, 0)
+    half = lax.rem(k + rep, 2)
+    for m in (0, 1, -1, 2):
+        i = spot(-m, 0, 0) + half
+        remote(feat_hbm.at[half], feat.at[0, i], x_send, f_recv.at[i], over(m)).start()
+    first_copy = pltpu.make_async_copy(feat_hbm, feat.at[0, pl.ds(0, 2)], first_sem)
+
+    @pl.when(native)
+    def _():
+        first_copy.start()
+        for m in (1, -1, 2):
+            for h in range(2):
+                i = spot(-m, 0, h)
+                remote(feat_hbm.at[h], feat.at[0, i], n_send, f_recv.at[i], near(m, 0)).start()
+        first_copy.wait()
+
+    @pl.when(jnp.logical_not(native))
+    def _():
+        for h in range(2):
+            wait_f(0, 0, h)
+
     for h in range(2):
         send_f(0, 0, h, 0, 1)
         send_f(0, 0, 1 - h, 0, -1)
@@ -164,16 +185,11 @@
     acc[...] = jnp.zeros_like(acc)
     tile_copy.wait()
     prep(0, 0)
-    wait_f(3, 0, 0)
-    send_f(3, 0, 0, 1, 0)
-    wait_f(1, 0, 1)
-    send_f(1, 0, 1, -1, 0)
-    wait_f(3, 0, 1)
-    wait_f(1, 0, 0)
     for da in (3, 1):
+        for h in range(2):
+            wait_f(da, 0, h)
         give_f(da, 0)
-    for h in range(2):
-        for da in (3, 1):
+        for h in range(2):
             send_f(da, 0, h, 0, 1)
             send_f(da, 0, 1 - h, 0, -1)
     prep(1, 0)
@@ -223,7 +239,6 @@
     multiply(1, 2)
 
     swap[0] = acc[:, 0:TILE] + acc[:, TILE : 2 * TILE]
-    twin = (blk, 1 - rep)
     c = remote(swap.at[0], swap.at[1], swap_send, swap_recv, twin)
     c.start()
     for l in loads:
@@ -281,6 +296,8 @@
         send_full(da, 1, 1, 0, 1)
         take_q(da, 3)
         send_full(da, 3, 0, 1, -1)
+
+    def step2_sums(da):
         for db, h, m in ((1, 0, 1), (3, 1, -1)):
             arrived(b_opp.at[da, h], bo_recv.at[da, h])
             i = spot(da, db, h)
@@ -295,10 +312,9 @@
         i = spot(da, 0, 0)
         part[0, i : i + 2] = part[0, i : i + 2] + (b_full[da, 0] + b_full[da, 1])
 
-    def send_a(da, h, n, m):
-        remote(
-            part.at[0, spot(da, 0, h)], a_full.at[n, h], af_send, af_recv.at[n, h], near(m, 0)
-        ).start()
+    def send_a(da, n, m):
+        i = spot(da, 0, 0)
+        remote(part.at[0, pl.ds(i, 2)], a_full.at[n], af_send, af_recv.at[n], near(m, 0)).start()
 
     def weight_term():
         agg_t[...] = (swap[0] + swap[1]).T
@@ -331,60 +347,41 @@
         for d in plane_peers:
             remote(wr3.at[here], wr3.at[here], w3_send, w3_recv, plane_dev(*d)).start()
 
-    back(1, 2)
-    give_q(2)
-    back(0, 2)
-    step1(2)
-    back(1, 1)
-    give_q(1)
-    step2(2)
-    back(0, 1)
-    step1(1)
-    back(1, 3)
-    give_q(3)
-    step2(1)
-    back(0, 3)
-    step1(3)
-    back(1, 0)
-    give_q(0)
-    step2(3)
-    back(0, 0)
-    step1(0)
-    step2(0)
+    for da in (2, 1, 3, 0):
+        back(1, da)
+        give_q(da)
+        back(0, da)
+        step1(da)
+        step2(da)
     weight_term()
+    for da in (2, 1, 3, 0):
+        step2_sums(da)
     step3(2)
-    for h, m in ((0, 1), (1, -1)):
-        remote(part.at[0, spot(2, 0, h)], a_opp.at[h], ao_send, ao_recv.at[h], near(m, 0)).start()
+    send_a(2, 2, 2)
+    weight_line()
     step3(1)
-    send_a(1, 1, 0, 1)
-    weight_line()
+    send_a(1, 0, 1)
     step3(3)
-    send_a(3, 0, 1, -1)
-    for da, h, m in ((1, 0, 1), (3, 1, -1)):
-        arrived(a_opp.at[h], ao_recv.at[h])
-        i = spot(da, 0, h)
-        part[0, i] = part[0, i] + a_opp[h]
-        send_a(da, h, h, m)
+    send_a(3, 1, -1)
     weight_plane()
     step3(0)
-    for n in range(2):
-        for h in range(2):
-            arrived(a_full.at[n, h], af_recv.at[n, h])
-    part[0, 0:2] = part[0, 0:2] + (a_full[0] + a_full[1])
+    for n in range(3):
+        arrived(a_full.at[n], af_recv.at[n])
+    part[0, 0:2] = part[0, 0:2] + (a_full[0] + a_full[1]) + a_full[2]
 
     total = part.at[0, pl.ds(0, 2)]
 
     @pl.when(native)
     def _():
-        remote(total, xr.at[1], t_send.at[0], t_recv.at[1], (at(y, z, xl, k), 1 - rep)).start()
+        remote(total, xr.at[1], t_send.at[0], t_recv.at[1], twin).start()
         arrived(xr.at[0], t_recv.at[0])
         fgv[...] = (part[0, 0:2] + xr[0]).reshape(TILE, 256).T
         sent(total, t_send.at[0])
 
     @pl.when(jnp.logical_not(native))
     def _():
-        remote(total, xr.at[0], t_send.at[0], t_recv.at[0], (at(y, z, 1 - xl, k), rep)).start()
-        remote(total, xr.at[0], t_send.at[1], t_recv.at[0], (at(y, z, 1 - xl, k), 1 - rep)).start()
+        remote(total, xr.at[0], t_send.at[0], t_recv.at[0], (at(y, z, 1 - xl, 1 - k), rep)).start()
+        remote(total, xr.at[0], t_send.at[1], t_recv.at[0], (at(y, z, 1 - xl, 1 - k), 1 - rep)).start()
         arrived(xr.at[0], t_recv.at[0])
         arrived(xr.at[1], t_recv.at[1])
         fgv[...] = (xr[0] + xr[1]).reshape(TILE, 256).T
@@ -404,14 +401,18 @@
     wg_copy = pltpu.make_async_copy(wgv, wgrad_hbm, store_sem.at[2])
     wg_copy.start()
 
-    sent(feat.at[0, half], x_send)
-    sent(feat.at[0, pl.ds(0, 30)], f_send)
+    sent(feat.at[0, pl.ds(0, 4)], x_send)
+
+    @pl.when(native)
+    def _():
+        sent(feat.at[0, pl.ds(0, 6)], n_send)
+
+    sent(feat.at[0, pl.ds(0, 24)], f_send)
     sent(feat.at[0], fs_send)
     sent(swap.at[0], swap_send)
     sent(part.at[1], q_send)
     sent(b_opp, bo_send)
     sent(b_full, bf_send)
-    sent(a_opp, ao_send)
     sent(a_full, af_send)
     sent(wr1, w1_send)
     sent(wr2.at[pl.ds(0, 7)], w2_send)
@@ -453,30 +454,28 @@
             vm((32, 64, 256), F32),
             vm((4, 2, 64, 256), F32),
             vm((4, 2, 2, 64, 256), F32),
-            vm((2, 64, 256), F32),
-            vm((2, 2, 64, 256), F32),
+            vm((3, 2, 64, 256), F32),
             vm((2, 2, 64, 256), F32),
             vm((256, TILE), F32),
             vm((16, 8, TILE), F32),
             vm((15, 8, TILE), F32),
             vm((8, 8, TILE), F32),
-            vm((8, TILE), F32),
             vm((16, 2, 8, TILE), F32),
             vm((TILE, 256), F32),
             dma, dma((2,)), dma, dma((3,)),
-            dma, dma((32,)), dma, dma((16,)), dma, dma((2,)), dma, dma,
-            dma, dma((16,)), dma, dma((4, 2)), dma, dma((4, 2, 2)), dma, dma((2,)), dma, dma((2, 2)),
+            dma, dma((32,)), dma, dma((16,)), dma, dma, dma, dma,
+            dma, dma((16,)), dma, dma((4, 2)), dma, dma((4, 2, 2)), dma, dma((3,)),
             dma((2,)), dma((2,)), dma, dma, dma, dma, dma, dma,
         ],
         compiler_params=pltpu.CompilerParams(
-            collective_id=0, has_side_effects=True, vmem_limit_bytes=48 * 1024 * 1024
+            collective_id=0, has_side_effects=True, vmem_limit_bytes=60 * 1024 * 1024
         ),
         cost_estimate=pl.CostEstimate(flops=3_000_000_000, bytes_accessed=8_000_000, transcendentals=65536),
     )(
         features.reshape(2, TILE, TILE),
         weight,
         tile_values.reshape(16, 2, 2, 3, TILE, TILE),
-        tile_pos,
+        tile_pos.transpose(2, 0, 1),
         tile_counts,
         out_grad,
     )

time: 84.6 us -> 68.9 us (0.81)
  the two profiles are of different devices: /device:TPU:2 before, /device:TPU:1 now
where the time goes in v2:
time: 68.9 us; the launch traced here: 68.6 us
  Pallas kernels  63.2 us (92%)
  local copies, waits for them, and re-layouts  4.8 us (7%)
    pallas_call x1, Pallas kernels, body(): pl.pallas_call(kernel, out_shape=(jax.ShapeDtypeStruct((256, 256), F32),...  63.2 us
    unnamed x3, local copies, waits for them, and re-layouts  4.8 us

profile of v2, /device:TPU:1, one launch (start us, length us, event | category | flops | bytes accessed | tf_op | source)
XLA Modules:
  0.0 68.6 jit_solution(2505557745697634184)
XLA Ops:
  0.6 63.2 %shard_map.85 = (f32[256,256]{1,0:T(8,128)}, f32[256,128]{1,0:T(8,128)}, f32[128,256]{1,0:T(8,128)}) custom-call(f32[2,128,128]{2,1,0:T(8,128)} %bitcast.4, f32[128,256]{1,0:T(8,128)} %weight_hbm.1, f32[16,2,2,3,128,128]{5,4,3,2,1,0:T(8,128)} %bitcast.3, s32[3,1,64]{2,1,0:T(1,128)} %bitcast.5, s32[1,64]{1,0:T(1,128)} %counts.1, f32[256,256]{1,0:T(8,128)} %ograd_hbm.1), custom_call_target="tpu_custom_call" | custom-call | flops 3000000000 | bytes 8000000 | tf_op jit(solution)/shard_map/pallas_call | solution.py:430
  63.8 1.7 %copy.12 = f32[256,256]{1,0:T(8,128)} copy(f32[256,256]{1,0:T(8,128)} %get-tuple-element.6) | data formatting | bytes 524288
  65.5 1.6 %copy.13 = f32[256,128]{1,0:T(8,128)} copy(f32[256,128]{1,0:T(8,128)} %get-tuple-element.7) | data formatting | bytes 262144
  67.1 1.6 %copy.14 = f32[128,256]{1,0:T(8,128)} copy(f32[128,256]{1,0:T(8,128)} %get-tuple-element.8) | data formatting | bytes 262144

commit v3 on v2

--- a/solution.py
+++ b/solution.py
@@ -21,11 +21,11 @@
 
 def kernel(
     feat_hbm, weight_hbm, tiles_hbm, pos, counts, ograd_hbm,
-    out_hbm, fgrad_hbm, wgrad_hbm,
-    tv, ah, al, feat, wside, acc, swap, agg_t, wt, og, pgrad, gs, outv,
-    part, sibq, b_opp, b_full, a_full, xr, fgv,
-    wg, wr1, wr2, wr3, wgv,
-    tile_sem, load_sem, first_sem, store_sem,
+    outv, fgv, wgv,
+    tv, ah, al, feat, wside, acc, swap, agg_t, wt, og, pgrad, gs,
+    part, sibq, b_opp, b_full, a_full, xr,
+    wg, wr1, wr2, wr3,
+    tile_sem, load_sem, first_sem,
     f_send, f_recv, fs_send, fs_recv, x_send, n_send, swap_send, swap_recv,
     q_send, q_recv, bo_send, bo_recv, bf_send, bf_recv, af_send, af_recv,
     t_send, t_recv, w1_send, w1_recv, w2_send, w2_recv, w3_send, w3_recv,
@@ -83,23 +83,21 @@
         pl.semaphore_signal(barrier, inc=1, device_id=dev, device_id_type=MESH)
 
     twin = (blk, 1 - rep)
-    peers = [near(1, 0), near(-1, 0), near(2, 0), near(0, 1), near(0, -1), sibling, twin]
+    peers = [near(2, 0), near(0, 2), twin, near(1, 0), near(-1, 0), near(0, 1), near(0, -1), sibling]
+    @pl.when(jnp.logical_not(native))
+    def _():
+        for m in (2, 1, -1):
+            for i in range(2):
+                greet(over_from(m, i))
+
+    for i in range(2):
+        greet((at(y, z, 1 - xl, 1 - k), i))
     for d in peers:
         greet(d)
-
-    for i in range(2):
-        greet((at(y, z, 1 - xl, 1 - k), i))
-
-    @pl.when(jnp.logical_not(native))
-    def _():
-        for m in (1, -1, 2):
-            for i in range(2):
-                greet(over_from(m, i))
-
     pl.semaphore_wait(barrier, len(peers) + 2 + 3)
 
     def spot(da, db, h):
-        return (da % 4 * 4 + db % 4) * 2 + h
+        return (db % 4 * 4 + da % 4) * 2 + h
 
     def send_f(da, db, h, ma, mb):
         there = spot(da - ma, db - mb, h)
@@ -117,8 +115,8 @@
             feat.at[0, pl.ds(i, 2)], feat.at[1, pl.ds(i, 2)], fs_send, fs_recv.at[i // 2], sibling
         ).start()
 
-    def prep(kk, da):
-        def one(db, carry):
+    def prep(kk, db):
+        def one(da, carry):
             if kk == 0:
                 own = k
             else:
@@ -135,7 +133,7 @@
                 live = ((p[0] == q) & (n > 0)) | ((p[1] == q) & (n > 1)) | ((p[2] == q) & (n > 2))
                 t = tv[base, xx, s] * jnp.where(live, 1.0, 0.0).astype(F32)
                 hi, lo = split(t)
-                col = pl.multiple_of((kk * 16 + da * 4 + db) * 256 + q % 2 * TILE, TILE)
+                col = pl.multiple_of((kk * 16 + db * 4 + da) * 256 + q % 2 * TILE, TILE)
                 rows = slice(q // 2 * TILE, (q // 2 + 1) * TILE)
                 ah[rows, pl.ds(col, TILE)] = hi
                 al[rows, pl.ds(col, TILE)] = lo
@@ -143,23 +141,18 @@
 
         lax.fori_loop(0, 4, one, 0)
 
-    def multiply(kk, da):
-        hi, lo = split(feat[kk, da * 8 : da * 8 + 8].reshape(1024, TILE))
+    def multiply(kk, db):
+        hi, lo = split(feat[kk, db * 8 : db * 8 + 8].reshape(1024, TILE))
         wside[:, 0:TILE] = hi
         wside[:, TILE : 2 * TILE] = lo
-        cols = slice((kk * 16 + da * 4) * 256, (kk * 16 + da * 4 + 4) * 256)
+        cols = slice((kk * 16 + db * 4) * 256, (kk * 16 + db * 4 + 4) * 256)
         w = wside[...]
         acc[...] += jnp.dot(ah[:, cols], w, preferred_element_type=F32) + jnp.dot(
             al[:, cols], w, preferred_element_type=F32
         )
 
-    def sib_group(da):
-        for db in range(4):
-            i = da * 4 + db
-            arrived(feat.at[1, pl.ds(2 * i, 2)], fs_recv.at[i])
-
     half = lax.rem(k + rep, 2)
-    for m in (0, 1, -1, 2):
+    for m in (0, 2, 1, -1):
         i = spot(-m, 0, 0) + half
         remote(feat_hbm.at[half], feat.at[0, i], x_send, f_recv.at[i], over(m)).start()
     first_copy = pltpu.make_async_copy(feat_hbm, feat.at[0, pl.ds(0, 2)], first_sem)
@@ -167,7 +160,7 @@
     @pl.when(native)
     def _():
         first_copy.start()
-        for m in (1, -1, 2):
+        for m in (2, 1, -1):
             for h in range(2):
                 i = spot(-m, 0, h)
                 remote(feat_hbm.at[h], feat.at[0, i], n_send, f_recv.at[i], near(m, 0)).start()
@@ -178,65 +171,62 @@
         for h in range(2):
             wait_f(0, 0, h)
 
-    for h in range(2):
-        send_f(0, 0, h, 0, 1)
-        send_f(0, 0, 1 - h, 0, -1)
-    give_f(0, 0)
+    def spread(da):
+        for h in range(2):
+            send_f(da, 0, h, 0, 1)
+            send_f(da, 0, 1 - h, 0, -1)
+        give_f(da, 0)
+
+    def pass_on(da):
+        for h, db, m in ((0, 3, 1), (1, 1, -1)):
+            wait_f(da, db, h)
+            send_f(da, db, h, 0, m)
+        for h, db in ((1, 3), (0, 1)):
+            wait_f(da, db, h)
+            give_f(da, db)
+
+    def finish(da):
+        for h in range(2):
+            wait_f(da, 2, h)
+        give_f(da, 2)
+
+    def sib_multiply(db):
+        for da in range(4):
+            i = spot(da, db, 0)
+            arrived(feat.at[1, pl.ds(i, 2)], fs_recv.at[i // 2])
+        multiply(1, db)
+
+    spread(0)
     acc[...] = jnp.zeros_like(acc)
     tile_copy.wait()
     prep(0, 0)
-    for da in (3, 1):
+    for da in (2, 3, 1):
         for h in range(2):
             wait_f(da, 0, h)
-        give_f(da, 0)
-        for h in range(2):
-            send_f(da, 0, h, 0, 1)
-            send_f(da, 0, 1 - h, 0, -1)
+        spread(da)
     prep(1, 0)
-    wait_f(0, 3, 0)
-    send_f(0, 3, 0, 0, 1)
-    wait_f(0, 1, 1)
-    send_f(0, 1, 1, 0, -1)
-    wait_f(2, 0, 0)
-    wait_f(2, 0, 1)
-    give_f(2, 0)
-    for h in range(2):
-        send_f(2, 0, h, 0, 1)
-        send_f(2, 0, 1 - h, 0, -1)
-    wait_f(0, 3, 1)
-    give_f(0, 3)
-    wait_f(0, 1, 0)
-    give_f(0, 1)
     prep(0, 3)
-    for da in (3, 1, 2):
-        wait_f(da, 3, 0)
-        send_f(da, 3, 0, 0, 1)
-        wait_f(da, 1, 1)
-        send_f(da, 1, 1, 0, -1)
-        wait_f(da, 3, 1)
-        give_f(da, 3)
-        wait_f(da, 1, 0)
-        give_f(da, 1)
-        before = {3: 0, 1: 3, 2: 1}[da]
-        wait_f(before, 2, 0)
-        wait_f(before, 2, 1)
-        give_f(before, 2)
-        if da == 3:
-            prep(1, 3)
-            prep(0, 1)
-        if da == 1:
-            prep(1, 1)
-            prep(0, 2)
-            prep(1, 2)
-        multiply(0, before)
-        sib_group(before)
-        multiply(1, before)
-    wait_f(2, 2, 0)
-    wait_f(2, 2, 1)
-    give_f(2, 2)
+    pass_on(0)
+    prep(0, 1)
+    multiply(0, 0)
+    pass_on(2)
+    sib_multiply(0)
+    pass_on(3)
+    prep(1, 3)
+    prep(1, 1)
+    pass_on(1)
+    multiply(0, 3)
+    finish(0)
+    multiply(0, 1)
+    prep(0, 2)
+    finish(2)
+    sib_multiply(3)
+    prep(1, 2)
+    finish(3)
+    sib_multiply(1)
+    finish(1)
     multiply(0, 2)
-    sib_group(2)
-    multiply(1, 2)
+    sib_multiply(2)
 
     swap[0] = acc[:, 0:TILE] + acc[:, TILE : 2 * TILE]
     c = remote(swap.at[0], swap.at[1], swap_send, swap_recv, twin)
@@ -255,20 +245,18 @@
     hi, lo = split(g_t)
     gs[0:TILE] = hi
     gs[TILE : 2 * TILE] = lo
-    out_copy = pltpu.make_async_copy(outv, out_hbm, store_sem.at[0])
-    out_copy.start()
-
-    def back(kk, da):
-        cols = slice((kk * 16 + da * 4) * 256, (kk * 16 + da * 4 + 4) * 256)
+
+    def back(kk, db):
+        cols = slice((kk * 16 + db * 4) * 256, (kk * 16 + db * 4 + 4) * 256)
         main = jnp.dot(gs[...], ah[:, cols], preferred_element_type=F32)
         rest = jnp.dot(gs[0:TILE], al[:, cols], preferred_element_type=F32)
         total = main[0:TILE] + main[TILE : 2 * TILE] + rest
-        for db in range(4):
+        for da in range(4):
             for h in range(2):
-                part[kk, spot(da, db, h)] = total[h * 64 : h * 64 + 64, db * 256 : db * 256 + 256]
-
-    def give_q(da):
-        for db in (2, 1, 3, 0):
+                part[kk, spot(da, db, h)] = total[h * 64 : h * 64 + 64, da * 256 : da * 256 + 256]
+
+    def give_q(db):
+        for da in (2, 1, 3, 0):
             i = spot(da, db, 0)
             remote(
                 part.at[1, pl.ds(i, 2)], sibq.at[pl.ds(i, 2)], q_send, q_recv.at[i // 2], sibling
@@ -291,11 +279,12 @@
             part.at[0, spot(da, db, h)], b_full.at[da, n, h], bf_send, bf_recv.at[da, n, h], near(0, m)
         ).start()
 
-    def step2(da):
-        take_q(da, 1)
-        send_full(da, 1, 1, 0, 1)
-        take_q(da, 3)
-        send_full(da, 3, 0, 1, -1)
+    def step2(da, db):
+        take_q(da, db)
+        if db == 1:
+            send_full(da, 1, 1, 0, 1)
+        else:
+            send_full(da, 3, 0, 1, -1)
 
     def step2_sums(da):
         for db, h, m in ((1, 0, 1), (3, 1, -1)):
@@ -347,13 +336,17 @@
         for d in plane_peers:
             remote(wr3.at[here], wr3.at[here], w3_send, w3_recv, plane_dev(*d)).start()
 
-    for da in (2, 1, 3, 0):
-        back(1, da)
-        give_q(da)
-        back(0, da)
-        step1(da)
-        step2(da)
-    weight_term()
+    for db in (2, 1, 3, 0):
+        back(1, db)
+        give_q(db)
+        back(0, db)
+        for da in (2, 1, 3, 0):
+            if db == 2:
+                step1(da)
+            elif db != 0:
+                step2(da, db)
+        if db == 3:
+            weight_term()
     for da in (2, 1, 3, 0):
         step2_sums(da)
     step3(2)
@@ -388,8 +381,6 @@
         sent(total, t_send.at[0])
         sent(total, t_send.at[1])
 
-    fg_copy = pltpu.make_async_copy(fgv, fgrad_hbm, store_sem.at[1])
-    fg_copy.start()
 
     arrived(wr3.at[pl.ds(0, 15)], w3_recv)
     for half_index in range(2):
@@ -398,8 +389,6 @@
                 wgv[half_index * 64 + i * 8 : half_index * 64 + i * 8 + 8, j * TILE : j * TILE + TILE] = wr3[
                     i * 2 + j, half_index
                 ]
-    wg_copy = pltpu.make_async_copy(wgv, wgrad_hbm, store_sem.at[2])
-    wg_copy.start()
 
     sent(feat.at[0, pl.ds(0, 4)], x_send)
 
@@ -417,9 +406,6 @@
     sent(wr1, w1_send)
     sent(wr2.at[pl.ds(0, 7)], w2_send)
     sent(wr3.at[pl.ds(0, 15)], w3_send)
-    out_copy.wait()
-    fg_copy.wait()
-    wg_copy.wait()
 
 
 def body(features, weight, tile_values, tile_pos, tile_counts, out_grad):
@@ -427,15 +413,17 @@
     vm = pltpu.VMEM
     any_space = pl.BlockSpec(memory_space=pl.ANY)
     smem = pl.BlockSpec(memory_space=pltpu.SMEM)
+    vspace = pl.BlockSpec(memory_space=pltpu.VMEM)
+    shapes = (
+        jax.ShapeDtypeStruct((256, 256), F32),
+        jax.ShapeDtypeStruct((256, 128), F32),
+        jax.ShapeDtypeStruct((128, 256), F32),
+    )
     return pl.pallas_call(
         kernel,
-        out_shape=(
-            jax.ShapeDtypeStruct((256, 256), F32),
-            jax.ShapeDtypeStruct((256, 128), F32),
-            jax.ShapeDtypeStruct((128, 256), F32),
-        ),
+        out_shape=tuple(pltpu.VMEM(x.shape, x.dtype) for x in shapes),
         in_specs=[any_space, any_space, any_space, smem, smem, any_space],
-        out_specs=(any_space, any_space, any_space),
+        out_specs=(vspace,) * 3,
         scratch_shapes=[
             vm((16, 2, 3, TILE, TILE), F32),
             vm((256, 8192), BF16),
@@ -449,20 +437,17 @@
             vm((256, 256), F32),
             vm((256, 256), F32),
             vm((256, 256), BF16),
-            vm((256, 256), F32),
             vm((2, 32, 64, 256), F32),
             vm((32, 64, 256), F32),
             vm((4, 2, 64, 256), F32),
             vm((4, 2, 2, 64, 256), F32),
             vm((3, 2, 64, 256), F32),
             vm((2, 2, 64, 256), F32),
-            vm((256, TILE), F32),
             vm((16, 8, TILE), F32),
             vm((15, 8, TILE), F32),
             vm((8, 8, TILE), F32),
             vm((16, 2, 8, TILE), F32),
-            vm((TILE, 256), F32),
-            dma, dma((2,)), dma, dma((3,)),
+            dma, dma((2,)), dma,
             dma, dma((32,)), dma, dma((16,)), dma, dma, dma, dma,
             dma, dma((16,)), dma, dma((4, 2)), dma, dma((4, 2, 2)), dma, dma((3,)),
             dma((2,)), dma((2,)), dma, dma, dma, dma, dma, dma,

time: 68.9 us -> 60.4 us (0.88)
  Pallas kernels: 63.2 us -> 57.6 us
  local copies, waits for them, and re-layouts: 4.8 us -> 2.01 us
    pallas_call x1, Pallas kernels: 63.2 us -> 57.6 us  [body(): pl.pallas_call(kernel, out_shape=tuple((pltpu.VMEM(x.shape, x.dtype) for...]
    unnamed x3, local copies, waits for them, and re-layouts: 4.8 us -> 2.01 us
where the time goes in v3:
time: 60.4 us; the launch traced here: 60.2 us
  Pallas kernels  57.6 us (95%)
  local copies, waits for them, and re-layouts  2.01 us (3%)
  between operations  0.64 us (1%)
    pallas_call x1, Pallas kernels, body(): pl.pallas_call(kernel, out_shape=tuple((pltpu.VMEM(x.shape, x.dtype) for...  57.6 us
    unnamed x3, local copies, waits for them, and re-layouts  2.01 us

profile of v3, /device:TPU:1, one launch (start us, length us, event | category | flops | bytes accessed | tf_op | source)
XLA Modules:
  0.0 60.2 jit_solution(5159218038885445135)
XLA Ops:
  0.6 57.6 %shard_map.85 = (f32[256,256]{1,0:T(8,128)S(1)}, f32[256,128]{1,0:T(8,128)S(1)}, f32[128,256]{1,0:T(8,128)S(1)}) custom-call(f32[2,128,128]{2,1,0:T(8,128)} %bitcast.4, f32[128,256]{1,0:T(8,128)} %weight_hbm.1, f32[16,2,2,3,128,128]{5,4,3,2,1,0:T(8,128)} %bitcast.3, s32[3,1,64]{2,1,0:T(1,128)} %bitcast.5, s32[1,64]{1,0:T(1,128)} %counts.1, f32[256,256]{1,0:T(8,128)} %ograd_hbm.1), custom_call_target="tpu_custom_call" | custom-call | flops 3000000000 | bytes 8000000 | tf_op jit(solution)/shard_map/pallas_call | solution.py:422
  58.2 0.7 %copy.12 = f32[256,256]{1,0:T(8,128)} copy(f32[256,256]{1,0:T(8,128)S(1)} %get-tuple-element.3) | data formatting | bytes 524288
  58.9 0.7 %copy.13 = f32[256,128]{1,0:T(8,128)} copy(f32[256,128]{1,0:T(8,128)S(1)} %get-tuple-element.4) | data formatting | bytes 262144
  59.6 0.7 %copy.14 = f32[128,256]{1,0:T(8,128)} copy(f32[128,256]{1,0:T(8,128)S(1)} %get-tuple-element.5) | data formatting | bytes 262144

commit v4 on v3

v4 whole, which is shorter than its diff:
```python
import math

import jax
import jax.numpy as jnp
from jax import lax
from jax.experimental import pallas as pl
from jax.experimental.pallas import tpu as pltpu
from jax.sharding import PartitionSpec as P

HIGHEST = lax.Precision.HIGHEST
MESH = pl.DeviceIdType.MESH
F32, BF16 = jnp.float32, jnp.bfloat16
NODES = 16384
TILE = 128


def split(x):
    hi = x.astype(BF16)
    return hi, (x - hi.astype(F32)).astype(BF16)


def kernel(
    feat_hbm, weight_hbm, tiles_hbm, pos_hbm, counts_hbm, ograd_hbm,
    outv, fgv, wgv,
    pos, counts, tv, ah, al, feat, wside, acc, swap, agg_t, wt, og, pgrad, gs,
    part, sibq, b_opp, b_full, a_full, xr,
    wg, wr1, wr2, wr3,
    tile_sem, load_sem, first_sem,
    f_send, f_recv, f2_recv, fs_send, fs_recv, x_send, n_send, swap_send, swap_recv,
    q_send, q_recv, bo_send, bo_recv, bf_send, bf_recv, af_send, af_recv,
    t_send, t_recv, w1_send, w1_recv, w2_send, w2_recv, w3_send, w3_recv,
):
    blk, rep = lax.axis_index("blk"), lax.axis_index("rep")
    y, z = lax.rem(lax.div(blk, 16), 4), lax.rem(lax.div(blk, 4), 4)
    xl, k = lax.rem(lax.div(blk, 2), 2), lax.rem(blk, 2)
    native = k == rep

    def at(yy, zz, xx, kk):
        return ((lax.rem(yy + 8, 4) * 4 + lax.rem(zz + 8, 4)) * 2 + xx) * 2 + kk

    def near(da, db):
        return (at(y + da * (1 - k) + db * k, z + da * k + db * (1 - k), xl, k), rep)

    sibling = (at(y, z, xl, 1 - k), rep)

    def remote(src, dst, ssem, rsem, dev):
        return pltpu.make_async_remote_copy(
            src_ref=src, dst_ref=dst, send_sem=ssem, recv_sem=rsem, device_id=dev, device_id_type=MESH
        )

    def arrived(dst, rsem):
        remote(dst, dst, rsem, rsem, sibling).wait_recv()

    def sent(src, ssem):
        remote(src, src, ssem, ssem, sibling).wait_send()

    tile_copy = pltpu.make_async_copy(tiles_hbm.at[:, :, rep], tv, tile_sem)
    tile_copy.start()
    loads = [
        pltpu.make_async_copy(weight_hbm, wt, load_sem.at[0]),
        pltpu.make_async_copy(ograd_hbm, og, load_sem.at[1]),
    ]
    places = [
        pltpu.make_async_copy(pos_hbm, pos, load_sem.at[2]),
        pltpu.make_async_copy(counts_hbm, counts, load_sem.at[3]),
    ]
    for c in places + loads:
        c.start()

    barrier = pltpu.get_barrier_semaphore()
    plane_peers = [(dy, dz) for dy in range(4) for dz in range(4) if (dy, dz) != (0, 0)]
    line_peers = [(i, j, l) for i in range(2) for j in range(2) for l in range(2) if (i, j, l) != (0, 0, 0)]

    def plane_dev(dy, dz):
        return (at(y + dy, z + dz, xl, k), rep)

    def line_dev(i, j, l):
        return (at(y, z, lax.rem(xl + j, 2), lax.rem(k + l, 2)), lax.rem(rep + i, 2))

    def near_in(u, mf, mg):
        return near(mf, mg) if u == 0 else near(mg, mf)

    half = lax.rem(k + rep, 2)
    along_y = k * (1 - half) + (1 - k) * half

    def over(m):
        return (at(y + m * along_y, z + m * (1 - along_y), 1 - xl, 1 - k), k)

    def over_from(m, i):
        u = lax.rem(1 - k + i, 2)
        c = (1 - k) * (1 - u) + k * u
        return (at(y + m * c, z + m * (1 - c), 1 - xl, 1 - k), i)

    def greet(dev):
        pl.semaphore_signal(barrier, inc=1, device_id=dev, device_id_type=MESH)

    twin = (blk, 1 - rep)
    peers = [near(2, 0), near(0, 2), twin, near(1, 0), near(-1, 0), near(0, 1), near(0, -1), sibling]
    @pl.when(jnp.logical_not(native))
    def _():
        for m in (2, 1, -1):
            for i in range(2):
                greet(over_from(m, i))

    for i in range(2):
        greet((at(y, z, 1 - xl, 1 - k), i))
    for d in peers:
        greet(d)
    pl.semaphore_wait(barrier, len(peers) + 2 + 3)

    def unit(u, f, g):
        return g % 4 * 8 + u * 4 + f % 4

    def wait_f(u, f, g):
        i = unit(u, f, g)
        arrived(feat.at[0, i], f_recv.at[i])

    def give_f(u, f, g):
        i = unit(u, f, g)
        remote(feat.at[0, i], feat.at[1, i], fs_send, fs_recv.at[i], sibling).start()

    def quarter(ref, q):
        return ref.at[pl.ds(q * 64, 64)]

    def prep(kk, g):
        own = k if kk == 0 else 1 - k
        xx = lax.rem(xl + own + rep, 2)

        def one(f, carry):
            for u in range(2):
                da, db = (f, g) if u == 0 else (g, f)
                yy = lax.rem(y + da * (1 - own) + db * own, 4)
                zz = lax.rem(z + da * own + db * (1 - own), 4)
                base = yy * 4 + zz
                c = (base * 2 + xx) * 2 + rep
                n = counts[0, c]
                p = [pos[s, 0, c] for s in range(3)]
                col = pl.multiple_of((kk * 32 + g * 8 + u * 4 + f) * TILE, TILE)
                for t in range(2):
                    q = t * 2 + u
                    s = jnp.where(p[0] == q, 0, jnp.where(p[1] == q, 1, 2))
                    live = ((p[0] == q) & (n > 0)) | ((p[1] == q) & (n > 1)) | ((p[2] == q) & (n > 2))
                    hi, lo = split(tv[base, xx, s] * jnp.where(live, 1.0, 0.0).astype(F32))
                    ah[t * TILE : (t + 1) * TILE, pl.ds(col, TILE)] = hi
                    al[t * TILE : (t + 1) * TILE, pl.ds(col, TILE)] = lo
            return carry

        lax.fori_loop(0, 4, one, 0)

    def multiply(kk, db, last=False):
        hi, lo = split(feat[kk, db * 8 : db * 8 + 8].reshape(1024, TILE))
        wside[:, 0:TILE] = hi
        wside[:, TILE : 2 * TILE] = lo
        cols = slice((kk * 16 + db * 4) * 256, (kk * 16 + db * 4 + 4) * 256)
        w = wside[...]
        for rows in (slice(0, TILE), slice(TILE, 2 * TILE)):
            new = acc[rows] + (
                jnp.dot(ah[rows, cols], w, preferred_element_type=F32)
                + jnp.dot(al[rows, cols], w, preferred_element_type=F32)
            )
            if last:
                swap[0, rows] = new[:, 0:TILE] + new[:, TILE : 2 * TILE]
                t = rows.start // TILE
                remote(swap.at[0, pl.ds(t * TILE, TILE)], swap.at[1, pl.ds(t * TILE, TILE)], swap_send,
                       swap_recv.at[t], twin).start()
            else:
                acc[rows] = new

    for m in (0, 2, 1, -1):
        i = half * 4 + (-m % 4)
        remote(feat_hbm.at[half], feat.at[0, i], x_send, f_recv.at[i], over(m)).start()
    first_copies = [pltpu.make_async_copy(feat_hbm.at[u], feat.at[0, u * 4], first_sem.at[u]) for u in range(2)]

    @pl.when(native)
    def _():
        for c in first_copies:
            c.start()
        for m in (2, 1, -1):
            for u in range(2):
                i = unit(u, -m, 0)
                remote(feat_hbm.at[u], feat.at[0, i], n_send, f_recv.at[i], near_in(u, m, 0)).start()
        for c in first_copies:
            c.wait()

    @pl.when(jnp.logical_not(native))
    def _():
        for u in range(2):
            wait_f(u, 0, 0)

    def spread(f):
        for u in range(2):
            if f != 0:
                wait_f(u, f, 0)
            for m in (1, -1):
                i = unit(u, f, -m)
                remote(feat.at[0, unit(u, f, 0)], feat.at[0, i], f_send, f_recv.at[i], near_in(u, 0, m)).start()
            give_f(u, f, 0)

    def pass_on(f):
        for u in range(2):
            i = unit(u, f, 2)
            for q, g, m, sem in ((0, 3, 1, f_recv.at[i]), (1, 1, -1, f2_recv.at[u * 4 + f])):
                wait_f(u, f, g)
                remote(
                    quarter(feat.at[0, unit(u, f, g)], q), quarter(feat.at[0, i], q), f_send, sem, near_in(u, 0, m)
                ).start()
                give_f(u, f, g)

    def finish(f):
        for u in range(2):
            i = unit(u, f, 2)
            arrived(quarter(feat.at[0, i], 0), f_recv.at[i])
            arrived(quarter(feat.at[0, i], 1), f2_recv.at[u * 4 + f])
            give_f(u, f, 2)

    def sib_multiply(g):
        for i in range(g * 8, g * 8 + 8):
            arrived(feat.at[1, i], fs_recv.at[i])
        multiply(1, g, g == 2)

    spread(0)
    acc[...] = jnp.zeros_like(acc)
    tile_copy.wait()
    for c in places:
        c.wait()
    prep(0, 0)
    for f in (2, 3, 1):
        spread(f)
    prep(1, 0)
    prep(0, 3)
    pass_on(0)
    prep(0, 1)
    multiply(0, 0)
    pass_on(2)
    sib_multiply(0)
    pass_on(3)
    prep(1, 3)
    prep(1, 1)
    pass_on(1)
    multiply(0, 3)
    finish(0)
    multiply(0, 1)
    prep(0, 2)
    finish(2)
    sib_multiply(3)
    prep(1, 2)
    finish(3)
    sib_multiply(1)
    finish(1)
    multiply(0, 2)
    sib_multiply(2)

    for l in loads:
        l.wait()
    w = wt[...]
    for t in range(2):
        rows = slice(t * TILE, t * TILE + TILE)
        arrived(swap.at[1, pl.ds(t * TILE, TILE)], swap_recv.at[t])
        agg = swap[0, rows] + swap[1, rows]
        pre = jnp.dot(agg, w, precision=HIGHEST, preferred_element_type=F32)
        gate = jax.nn.sigmoid(pre)
        outv[rows] = pre * gate
        pg = og[rows] * gate * (1.0 + pre * (1.0 - gate))
        pgrad[rows] = pg
        g_t = lax.dot_general(w, pg, (((1,), (1,)), ((), ())), precision=HIGHEST, preferred_element_type=F32)
        hi, lo = split(g_t)
        gs[0:TILE, rows] = hi
        gs[TILE : 2 * TILE, rows] = lo

    def back(kk, g):
        cols = slice((kk * 4 + g) * 1024, (kk * 4 + g + 1) * 1024)
        main = jnp.dot(gs[...], ah[:, cols], preferred_element_type=F32)
        rest = jnp.dot(gs[0:TILE], al[:, cols], preferred_element_type=F32)
        total = main[0:TILE] + main[TILE : 2 * TILE] + rest
        for i in range(8):
            part[kk, g * 8 + i] = total[:, i * TILE : i * TILE + TILE]

    def give_q(g):
        for f in (2, 1, 3, 0):
            for u in range(2):
                i = unit(u, f, g)
                remote(part.at[1, i], sibq.at[i], q_send, q_recv.at[i], sibling).start()

    def take_q(i):
        arrived(sibq.at[i], q_recv.at[i])
        part[0, i] = part[0, i] + sibq[i]

    def step1(u, f):
        i, j = unit(u, f, 2), u * 4 + f
        take_q(i)
        for q, m in ((0, 1), (1, -1)):
            remote(
                quarter(part.at[0, i], q), b_opp.at[q, j], bo_send, bo_recv.at[q, j], near_in(u, 0, m)
            ).start()

    def send_full(u, f, g, q):
        n, j = g // 2, u * 4 + f
        remote(
            quarter(part.at[0, unit(u, f, g)], q), quarter(b_full.at[n, j], q), bf_send, bf_recv.at[n, j, q],
            near_in(u, 0, 1 - 2 * n),
        ).start()

    def step2(u, f, g):
        take_q(unit(u, f, g))
        send_full(u, f, g, 1 - g // 2)

    def step2_sums(u, f):
        for q in range(2):
            g, j = 1 + 2 * q, u * 4 + f
            i, rows = unit(u, f, g), slice(q * 64, q * 64 + 64)
            arrived(b_opp.at[q, j], bo_recv.at[q, j])
            part[0, i, rows] = part[0, i, rows] + b_opp[q, j]
            send_full(u, f, g, q)

    def step3(u, f):
        i, j = unit(u, f, 0), u * 4 + f
        take_q(i)
        for n in range(2):
            for q in range(2):
                arrived(quarter(b_full.at[n, j], q), bf_recv.at[n, j, q])
        part[0, i] = part[0, i] + (b_full[0, j] + b_full[1, j])

    def send_a(u, f, n, m):
        remote(part.at[0, unit(u, f, 0)], a_full.at[n, u], af_send, af_recv.at[n, u], near_in(u, m, 0)).start()

    def weight_term():
        agg_t[...] = (swap[0] + swap[1]).T
        rows = agg_t[pl.ds(pl.multiple_of(rep * 64, 64), 64), :]
        term = jnp.dot(rows, pgrad[...], precision=HIGHEST, preferred_element_type=F32)
        for i in range(8):
            for j in range(2):
                wg[i * 2 + j] = term[i * 8 : i * 8 + 8, j * TILE : j * TILE + TILE]
        for dy, dz in plane_peers:
            there = lax.rem(y + dy, 4) * 4 + lax.rem(z + dz, 4)
            remote(wg.at[there], wr1.at[dy * 4 + dz - 1], w1_send, w1_recv, plane_dev(dy, dz)).start()

    here = y * 4 + z
    line = (rep * 2 + xl) * 2 + k

    def weight_line():
        arrived(wr1, w1_recv)
        total = wg[here]
        for i in range(15):
            total = total + wr1[i]
        wr2[line] = total
        for d in line_peers:
            remote(wr2.at[line], wr2.at[line], w2_send, w2_recv, line_dev(*d)).start()

    def weight_plane():
        arrived(wr2.at[pl.ds(0, 7)], w2_recv)
        for i in range(2):
            total = (wr2[4 * i] + wr2[4 * i + 1]) + (wr2[4 * i + 2] + wr2[4 * i + 3])
            wr3[here, i] = total * (1.0 / math.sqrt(NODES))
        for d in plane_peers:
            remote(wr3.at[here], wr3.at[here], w3_send, w3_recv, plane_dev(*d)).start()

    both = [(u, f) for f in (2, 1, 3, 0) for u in range(2)]
    for g in (2, 1, 3, 0):
        back(1, g)
        give_q(g)
        back(0, g)
        for u, f in both:
            if g == 2:
                step1(u, f)
            elif g != 0:
                step2(u, f, g)
        if g == 3:
            weight_term()
    for u, f in both:
        step2_sums(u, f)
    for f, n, m in ((2, 2, 2), (1, 0, 1), (3, 1, -1)):
        for u in range(2):
            step3(u, f)
            send_a(u, f, n, m)
        if f == 2:
            weight_line()
    weight_plane()
    for u in range(2):
        step3(u, 0)

    other = at(y, z, 1 - xl, 1 - k)
    for u in range(2):
        for n in range(3):
            arrived(a_full.at[n, u], af_recv.at[n, u])
        i = unit(u, 0, 0)
        part[0, i] = part[0, i] + (a_full[0, u] + a_full[1, u]) + a_full[2, u]
        total = part.at[0, i]

        @pl.when(native)
        def _():
            remote(total, xr.at[1, u], t_send.at[0], t_recv.at[1, u], twin).start()

        @pl.when(jnp.logical_not(native))
        def _():
            remote(total, xr.at[0, u], t_send.at[0], t_recv.at[0, u], (other, rep)).start()
            remote(total, xr.at[0, u], t_send.at[1], t_recv.at[0, u], (other, 1 - rep)).start()

    for u in range(2):
        arrived(xr.at[0, u], t_recv.at[0, u])

    @pl.when(native)
    def _():
        for u in range(2):
            fgv[u * TILE : (u + 1) * TILE] = (part[0, unit(u, 0, 0)] + xr[0, u]).T
        sent(xr.at[0], t_send.at[0])

    @pl.when(jnp.logical_not(native))
    def _():
        for u in range(2):
            arrived(xr.at[1, u], t_recv.at[1, u])
            fgv[u * TILE : (u + 1) * TILE] = (xr[1, u] + xr[0, u]).T
        sent(xr.at[0], t_send.at[0])
        sent(xr.at[0], t_send.at[1])

    arrived(wr3.at[pl.ds(0, 15)], w3_recv)
    for half_index in range(2):
        for i in range(8):
            for j in range(2):
                wgv[half_index * 64 + i * 8 : half_index * 64 + i * 8 + 8, j * TILE : j * TILE + TILE] = wr3[
                    i * 2 + j, half_index
                ]

    sent(feat.at[0, pl.ds(0, 4)], x_send)

    @pl.when(native)
    def _():
        sent(feat.at[0, pl.ds(0, 6)], n_send)

    sent(feat.at[0, pl.ds(0, 24)], f_send)
    sent(feat.at[0], fs_send)
    sent(swap.at[0], swap_send)
    sent(part.at[1], q_send)
    sent(b_opp, bo_send)
    sent(b_full, bf_send)
    sent(a_full, af_send)
    sent(wr1, w1_send)
    sent(wr2.at[pl.ds(0, 7)], w2_send)
    sent(wr3.at[pl.ds(0, 15)], w3_send)


def body(features, weight, tile_values, tile_pos, tile_counts, out_grad):
    dma = pltpu.SemaphoreType.DMA
    vm = pltpu.VMEM
    any_space = pl.BlockSpec(memory_space=pl.ANY)
    vspace = pl.BlockSpec(memory_space=pltpu.VMEM)
    shapes = (
        jax.ShapeDtypeStruct((256, 256), F32),
        jax.ShapeDtypeStruct((256, 128), F32),
        jax.ShapeDtypeStruct((128, 256), F32),
    )
    return pl.pallas_call(
        kernel,
        out_shape=tuple(pltpu.VMEM(x.shape, x.dtype) for x in shapes),
        in_specs=[any_space] * 6,
        out_specs=(vspace,) * 3,
        scratch_shapes=[
            pltpu.SMEM((3, 1, 64), jnp.int32),
            pltpu.SMEM((1, 64), jnp.int32),
            vm((16, 2, 3, TILE, TILE), F32),
            vm((256, 8192), BF16),
            vm((256, 8192), BF16),
            vm((2, 32, TILE, TILE), F32),
            vm((1024, 256), BF16),
            vm((256, 256), F32),
            vm((2, 256, TILE), F32),
            vm((TILE, 256), F32),
            vm((TILE, 256), F32),
            vm((256, 256), F32),
            vm((256, 256), F32),
            vm((256, 256), BF16),
            vm((2, 32, TILE, TILE), F32),
            vm((32, TILE, TILE), F32),
            vm((2, 8, 64, TILE), F32),
            vm((2, 8, TILE, TILE), F32),
            vm((3, 2, TILE, TILE), F32),
            vm((2, 2, TILE, TILE), F32),
            vm((16, 8, TILE), F32),
            vm((15, 8, TILE), F32),
            vm((8, 8, TILE), F32),
            vm((16, 2, 8, TILE), F32),
            dma, dma((4,)), dma((2,)),
            dma, dma((32,)), dma((8,)), dma, dma((32,)), dma, dma, dma, dma((2,)),
            dma, dma((32,)), dma, dma((2, 8)), dma, dma((2, 8, 2)), dma, dma((3, 2)),
            dma((2,)), dma((2, 2)), dma, dma, dma, dma, dma, dma,
        ],
        compiler_params=pltpu.CompilerParams(
            collective_id=0, has_side_effects=True, vmem_limit_bytes=60 * 1024 * 1024
        ),
        cost_estimate=pl.CostEstimate(flops=3_000_000_000, bytes_accessed=8_000_000, transcendentals=65536),
    )(
        features.reshape(2, TILE, TILE),
        weight,
        tile_values.reshape(16, 2, 2, 3, TILE, TILE),
        tile_pos.transpose(2, 0, 1),
        tile_counts,
        out_grad,
    )


def solution(mesh):
    return jax.shard_map(
        body,
        mesh=mesh,
        in_specs=(
            P("blk", None),
            P(),
            P("blk", None, None, None, None),
            P("blk", None, None),
            P("blk", None),
            P("blk", None),
        ),
        out_specs=(P("blk", None), P("blk", None), P()),
        check_vma=False,
    )
```

time: 60.4 us -> 58.1 us (0.962)
  Pallas kernels: 57.6 us -> 55.2 us
    pallas_call x1, Pallas kernels: 57.6 us -> 55.2 us  [body(): pl.pallas_call(kernel, out_shape=tuple((pltpu.VMEM(x.shape, x.dtype) for...]
where the time goes in v4:
time: 58.1 us; the launch traced here: 57.9 us
  Pallas kernels  55.2 us (95%)
  local copies, waits for them, and re-layouts  2.01 us (3%)
  between operations  0.64 us (1%)
    pallas_call x1, Pallas kernels, body(): pl.pallas_call(kernel, out_shape=tuple((pltpu.VMEM(x.shape, x.dtype) for...  55.2 us
    unnamed x3, local copies, waits for them, and re-layouts  2.01 us

profile of v4, /device:TPU:1, one launch (start us, length us, event | category | flops | bytes accessed | tf_op | source)
XLA Modules:
  0.0 57.9 jit_solution(1134897772937176447)
XLA Ops:
  0.6 55.2 %shard_map.85 = (f32[256,256]{1,0:T(8,128)S(1)}, f32[256,128]{1,0:T(8,128)S(1)}, f32[128,256]{1,0:T(8,128)S(1)}) custom-call(f32[2,128,128]{2,1,0:T(8,128)} %bitcast.4, f32[128,256]{1,0:T(8,128)} %weight_hbm.1, f32[16,2,2,3,128,128]{5,4,3,2,1,0:T(8,128)} %bitcast.3, s32[3,1,64]{2,1,0:T(1,128)} %bitcast.5, s32[1,64]{1,0:T(1,128)} %counts_hbm.1, ...), custom_call_target="tpu_custom_call" | custom-call | flops 3000000000 | bytes 8000000 | tf_op jit(solution)/shard_map/pallas_call | solution.py:451
  55.9 0.7 %copy.12 = f32[256,256]{1,0:T(8,128)} copy(f32[256,256]{1,0:T(8,128)S(1)} %get-tuple-element.3) | data formatting | bytes 524288
  56.6 0.7 %copy.13 = f32[256,128]{1,0:T(8,128)} copy(f32[256,128]{1,0:T(8,128)S(1)} %get-tuple-element.4) | data formatting | bytes 262144
  57.2 0.7 %copy.14 = f32[128,256]{1,0:T(8,128)} copy(f32[128,256]{1,0:T(8,128)S(1)} %get-tuple-element.5) | data formatting | bytes 262144

commit v5 on v4

--- a/solution.py
+++ b/solution.py
@@ -201,10 +201,26 @@
             i = unit(u, f, 2)
             for q, g, m, sem in ((0, 3, 1, f_recv.at[i]), (1, 1, -1, f2_recv.at[u * 4 + f])):
                 wait_f(u, f, g)
-                remote(
+                relay = remote(
                     quarter(feat.at[0, unit(u, f, g)], q), quarter(feat.at[0, i], q), f_send, sem, near_in(u, 0, m)
-                ).start()
+                )
+                if f == 2:
+                    relay.start()
+                else:
+                    pl.when(native)(relay.start)
                 give_f(u, f, g)
+
+    pair = (at(y, z, 1 - xl, 1 - k), rep)
+
+    def across(f):
+        @pl.when(native)
+        def _():
+            for u in range(2):
+                i = unit(u, f, 2)
+                for q, sem in ((0, f_recv.at[i]), (1, f2_recv.at[u * 4 + f])):
+                    remote(
+                        quarter(feat.at[0, unit(u, 2, f)], q), quarter(feat.at[0, i], q), f_send, sem, pair
+                    ).start()
 
     def finish(f):
         for u in range(2):
@@ -226,12 +242,16 @@
     prep(0, 0)
     for f in (2, 3, 1):
         spread(f)
+        if f == 2:
+            across(0)
     prep(1, 0)
     prep(0, 3)
     pass_on(0)
     prep(0, 1)
     multiply(0, 0)
     pass_on(2)
+    across(3)
+    across(1)
     sib_multiply(0)
     pass_on(3)
     prep(1, 3)
@@ -366,7 +386,9 @@
                 step2(u, f, g)
         if g == 3:
             weight_term()
-    for u, f in both:
+            for u in range(2):
+                step2_sums(u, 2)
+    for u, f in both[2:]:
         step2_sums(u, f)
     for f, n, m in ((2, 2, 2), (1, 0, 1), (3, 1, -1)):
         for u in range(2):
@@ -425,8 +447,12 @@
     @pl.when(native)
     def _():
         sent(feat.at[0, pl.ds(0, 6)], n_send)
-
-    sent(feat.at[0, pl.ds(0, 24)], f_send)
+        sent(feat.at[0, pl.ds(0, 30)], f_send)
+
+    @pl.when(jnp.logical_not(native))
+    def _():
+        sent(feat.at[0, pl.ds(0, 18)], f_send)
+
     sent(feat.at[0], fs_send)
     sent(swap.at[0], swap_send)
     sent(part.at[1], q_send)

time: 58.1 us -> 57.4 us (0.988)
  Pallas kernels: 55.2 us -> 54.6 us
    pallas_call x1, Pallas kernels: 55.2 us -> 54.6 us  [body(): pl.pallas_call(kernel, out_shape=tuple((pltpu.VMEM(x.shape, x.dtype) for...]
where the time goes in v5:
time: 57.4 us; the launch traced here: 57.3 us
  Pallas kernels  54.6 us (95%)
  local copies, waits for them, and re-layouts  2.01 us (4%)
  between operations  0.64 us (1%)
    pallas_call x1, Pallas kernels, body(): pl.pallas_call(kernel, out_shape=tuple((pltpu.VMEM(x.shape, x.dtype) for...  54.6 us
    unnamed x3, local copies, waits for them, and re-layouts  2.01 us

profile of v5, /device:TPU:1, one launch (start us, length us, event | category | flops | bytes accessed | tf_op | source)
XLA Modules:
  0.0 57.3 jit_solution(6010600426806898677)
XLA Ops:
  0.6 54.6 %shard_map.85 = (f32[256,256]{1,0:T(8,128)S(1)}, f32[256,128]{1,0:T(8,128)S(1)}, f32[128,256]{1,0:T(8,128)S(1)}) custom-call(f32[2,128,128]{2,1,0:T(8,128)} %bitcast.4, f32[128,256]{1,0:T(8,128)} %weight_hbm.1, f32[16,2,2,3,128,128]{5,4,3,2,1,0:T(8,128)} %bitcast.3, s32[3,1,64]{2,1,0:T(1,128)} %bitcast.5, s32[1,64]{1,0:T(1,128)} %counts_hbm.1, ...), custom_call_target="tpu_custom_call" | custom-call | flops 3000000000 | bytes 8000000 | tf_op jit(solution)/shard_map/pallas_call | solution.py:477
  55.2 0.7 %copy.12 = f32[256,256]{1,0:T(8,128)} copy(f32[256,256]{1,0:T(8,128)S(1)} %get-tuple-element.3) | data formatting | bytes 524288
  55.9 0.7 %copy.13 = f32[256,128]{1,0:T(8,128)} copy(f32[256,128]{1,0:T(8,128)S(1)} %get-tuple-element.4) | data formatting | bytes 262144
  56.6 0.7 %copy.14 = f32[128,256]{1,0:T(8,128)} copy(f32[128,256]{1,0:T(8,128)S(1)} %get-tuple-element.5) | data formatting | bytes 262144

commit v6 on v5

--- a/solution.py
+++ b/solution.py
@@ -166,6 +166,13 @@
             else:
                 acc[rows] = new
 
+    def spread_from(source, u, f):
+        for m in (1, -1):
+            i = unit(u, f, -m)
+            remote(source, feat.at[0, i], f_send, f_recv.at[i], near_in(u, 0, m)).start()
+        i = unit(u, f, 0)
+        remote(source, feat.at[1, i], fs_send, fs_recv.at[i], sibling).start()
+
     for m in (0, 2, 1, -1):
         i = half * 4 + (-m % 4)
         remote(feat_hbm.at[half], feat.at[0, i], x_send, f_recv.at[i], over(m)).start()
@@ -179,22 +186,19 @@
             for u in range(2):
                 i = unit(u, -m, 0)
                 remote(feat_hbm.at[u], feat.at[0, i], n_send, f_recv.at[i], near_in(u, m, 0)).start()
-        for c in first_copies:
-            c.wait()
+        for u in range(2):
+            spread_from(feat_hbm.at[u], u, 0)
 
     @pl.when(jnp.logical_not(native))
     def _():
         for u in range(2):
             wait_f(u, 0, 0)
+            spread_from(feat.at[0, unit(u, 0, 0)], u, 0)
 
     def spread(f):
         for u in range(2):
-            if f != 0:
-                wait_f(u, f, 0)
-            for m in (1, -1):
-                i = unit(u, f, -m)
-                remote(feat.at[0, unit(u, f, 0)], feat.at[0, i], f_send, f_recv.at[i], near_in(u, 0, m)).start()
-            give_f(u, f, 0)
+            wait_f(u, f, 0)
+            spread_from(feat.at[0, unit(u, f, 0)], u, f)
 
     def pass_on(f):
         for u in range(2):
@@ -234,7 +238,6 @@
             arrived(feat.at[1, i], fs_recv.at[i])
         multiply(1, g, g == 2)
 
-    spread(0)
     acc[...] = jnp.zeros_like(acc)
     tile_copy.wait()
     for c in places:
@@ -248,6 +251,12 @@
     prep(0, 3)
     pass_on(0)
     prep(0, 1)
+
+    @pl.when(native)
+    def _():
+        for c in first_copies:
+            c.wait()
+
     multiply(0, 0)
     pass_on(2)
     across(3)

time: 57.4 us -> 57.2 us (level)
  no operation moved by 1% of the time
where the time goes in v6:
time: 57.2 us; the launch traced here: 57.1 us
  Pallas kernels  54.4 us (95%)
  local copies, waits for them, and re-layouts  2.01 us (4%)
  between operations  0.64 us (1%)
    pallas_call x1, Pallas kernels, body(): pl.pallas_call(kernel, out_shape=tuple((pltpu.VMEM(x.shape, x.dtype) for...  54.4 us
    unnamed x3, local copies, waits for them, and re-layouts  2.01 us

profile of v6, /device:TPU:1, one launch (start us, length us, event | category | flops | bytes accessed | tf_op | source)
XLA Modules:
  0.0 57.1 jit_solution(7582525077077132812)
XLA Ops:
  0.6 54.4 %shard_map.85 = (f32[256,256]{1,0:T(8,128)S(1)}, f32[256,128]{1,0:T(8,128)S(1)}, f32[128,256]{1,0:T(8,128)S(1)}) custom-call(f32[2,128,128]{2,1,0:T(8,128)} %bitcast.4, f32[128,256]{1,0:T(8,128)} %weight_hbm.1, f32[16,2,2,3,128,128]{5,4,3,2,1,0:T(8,128)} %bitcast.3, s32[3,1,64]{2,1,0:T(1,128)} %bitcast.5, s32[1,64]{1,0:T(1,128)} %counts_hbm.1, ...), custom_call_target="tpu_custom_call" | custom-call | flops 3000000000 | bytes 8000000 | tf_op jit(solution)/shard_map/pallas_call | solution.py:486
  55.1 0.7 %copy.12 = f32[256,256]{1,0:T(8,128)} copy(f32[256,256]{1,0:T(8,128)S(1)} %get-tuple-element.3) | data formatting | bytes 524288
  55.8 0.7 %copy.13 = f32[256,128]{1,0:T(8,128)} copy(f32[256,128]{1,0:T(8,128)S(1)} %get-tuple-element.4) | data formatting | bytes 262144
  56.4 0.7 %copy.14 = f32[128,256]{1,0:T(8,128)} copy(f32[128,256]{1,0:T(8,128)S(1)} %get-tuple-element.5) | data formatting | bytes 262144
